TPU v7x, 256 devices: a whole 4x4x8 slice. The times are simulated.
256 devices in a mesh: space: 16 (over x, z_hi), mode: 16 (over y, z_lo, core).
Axes of the slice: x: 4, y: 4, z: 8 (z_hi: 4, z_lo: 2; z = z_hi * 2 + z_lo), core: 2. Of those that a mesh axis runs over, the one named last changes fastest.
Arguments:
- dist: bfloat16 [256, 2, 256, 576], P('mode', None, 'space')
- relax: float32 [2, 256], P(None, 'space'), may hold values from 0.1 to 0.9
- flags: int32 [2, 256], P(None, 'space'), may hold values from 0 to 2
- solid: int32 [2, 256], replicated, may hold values from 0 to 1, as said below
- inflow: bfloat16 [256, 576], P('mode'), may hold values from -2 to 2
- basis: bfloat16 [256, 256], replicated, as said below
- projection: bfloat16 [256, 256], replicated, may hold values from -0.375 to 0.375
Outputs:
- advanced: bfloat16 [256, 2, 256, 576], P('mode', None, 'space')
Inputs may be any that keep to these rules, and one draw needn't show every extreme that they name: `solid`: 1 marks the cells of a disc whose centre lies in the band. `basis`: column 0 is all ones.
All inputs are finite; a program needn't handle non-finite values.
Results may differ from a plain program's by a relative error of at most 0.006.
The roundings to bfloat16 on the way count: a program that leaves them out, or rounds other values in their place, can miss the bound.
Values may be sent and summed in bfloat16 or wider, within the bound.
No kernel may reach another device: no remote copies, remote signals or barrier semaphores. Data moves between devices by JAX's collectives and lax.ppermute only.
A program may use at most 64 MiB of HBM per device.

v0:
```python
import math

import jax
import jax.numpy as jnp
from jax import lax
from jax.sharding import PartitionSpec as P

VX = 24


VMAX = 4.6
DT_DX = 0.09
RHO_FLOOR = 0.3
TEMP_FLOOR = 0.2


def extended(cells, sides, width):
    for axis, dim in sides:
        count = lax.axis_size(axis)
        ends = count - 1
        head = lax.slice_in_dim(cells, 0, width, axis=dim)
        tail = lax.slice_in_dim(cells, cells.shape[dim] - width, cells.shape[dim], axis=dim)
        cells = jnp.concatenate(
            [
                lax.ppermute(tail, axis, [(i, (i + 1) % count) for i in range(ends)]),
                cells,
                lax.ppermute(head, axis, [((i + 1) % count, i) for i in range(ends)]),
            ],
            axis=dim,
        )
    return cells


def velocities(count):
    index = jnp.arange(count * count)
    step = 2.0 * VMAX / (count - 1)
    velocity_horizontal = -VMAX + step * (index // count).astype(jnp.float32)
    velocity_vertical = -VMAX + step * (index % count).astype(jnp.float32)
    return (velocity_horizontal, velocity_vertical, step * step)


def mirror_table(count, along_first):
    index = jnp.arange(count * count)
    first = index // count
    second = index % count
    if along_first:
        target = (count - 1 - first) * count + second
    else:
        target = first * count + (count - 1 - second)
    return (target[:, None] == index[None, :]).astype(jnp.bfloat16)


def maxwell(rho, mx, my, en, velocity_horizontal, velocity_vertical):
    safe = jnp.maximum(rho, RHO_FLOOR)
    ux = mx / safe
    uy = my / safe
    temp = jnp.maximum(en / safe - 0.5 * (ux * ux + uy * uy), TEMP_FLOOR)
    arg = (
        (velocity_horizontal - ux[..., None]) ** 2 + (velocity_vertical - uy[..., None]) ** 2
    ) / (2.0 * temp[..., None])
    return (safe / (2.0 * math.pi * temp))[..., None] * jnp.exp(-arg)


def velocity_moments(density_field, velocity_horizontal, velocity_vertical, quadrature_weight):
    rho = quadrature_weight * jnp.sum(density_field, -1)
    mx = quadrature_weight * jnp.sum(density_field * velocity_horizontal, -1)
    my = quadrature_weight * jnp.sum(density_field * velocity_vertical, -1)
    en = quadrature_weight * jnp.sum(
        density_field
        * (
            0.5
            * (velocity_horizontal * velocity_horizontal + velocity_vertical * velocity_vertical)
        ),
        -1,
    )
    return (rho, mx, my, en)


def heun_update(
    padded_state,
    collision_term,
    relax,
    flags,
    padded_solid,
    inflow,
    first_column,
    column_total,
    velocity_horizontal,
    velocity_vertical,
    table_first,
    table_second,
):
    state_half = padded_state[:, :, 1:-1]
    local_rows = state_half.astype(jnp.float32)
    left = padded_state[:, :, :-2].astype(jnp.float32)
    right = padded_state[:, :, 2:].astype(jnp.float32)
    rows = local_rows.shape[1]
    cols = local_rows.shape[2]
    bounce = jnp.flip(state_half, -1).astype(jnp.float32)
    inflow4 = inflow.astype(jnp.float32)[:, None, None, :]
    flag4 = flags[None, :, :, None]
    mirror_second = jnp.einsum(
        "krcv,vw->krcw", state_half, table_second, preferred_element_type=jnp.float32
    )
    edge_y = jnp.where(flag4 == 0, local_rows, jnp.where(flag4 == 1, inflow4, mirror_second))
    end_half = jnp.concatenate([state_half[:, :, :1], state_half[:, :, cols - 1 :]], 2)
    end_rows = end_half.astype(jnp.float32)
    end_flags = jnp.concatenate([flags[:, :1], flags[:, cols - 1 :]], 1)[None, :, :, None]
    mirror_first = jnp.einsum(
        "krcv,vw->krcw", end_half, table_first, preferred_element_type=jnp.float32
    )
    edge_ends = jnp.where(
        end_flags == 0, end_rows, jnp.where(end_flags == 1, inflow4, mirror_first)
    )
    solid_left = (padded_solid[:, :-2] == 1)[None, :, :, None]
    solid_right = (padded_solid[:, 2:] == 1)[None, :, :, None]
    left_val = jnp.where(solid_left, bounce, left)
    right_val = jnp.where(solid_right, bounce, right)
    left_first = jnp.where(first_column == 0, edge_ends[:, :, 0], left_val[:, :, 0])
    left_val = left_val.at[:, :, 0].set(left_first)
    right_last = jnp.where(
        first_column + cols == column_total, edge_ends[:, :, 1], right_val[:, :, cols - 1]
    )
    right_val = right_val.at[:, :, cols - 1].set(right_last)
    up_x = jnp.where(velocity_horizontal > 0, left_val, right_val)
    zero_row = jnp.zeros_like(local_rows[:, :1])
    below = jnp.concatenate([zero_row, local_rows[:, :-1]], 1)
    above = jnp.concatenate([local_rows[:, 1:], zero_row], 1)
    solid_own = padded_solid[:, 1:-1]
    zero_mask = jnp.zeros((1, cols), solid_own.dtype)
    solid_below = (jnp.concatenate([zero_mask, solid_own[:-1]], 0) == 1)[None, :, :, None]
    solid_above = (jnp.concatenate([solid_own[1:], zero_mask], 0) == 1)[None, :, :, None]
    row_index = jnp.arange(rows)
    out_below = (row_index == 0)[None, :, None, None]
    out_above = (row_index == rows - 1)[None, :, None, None]
    below_val = jnp.where(out_below, edge_y, jnp.where(solid_below, bounce, below))
    above_val = jnp.where(out_above, edge_y, jnp.where(solid_above, bounce, above))
    up_y = jnp.where(velocity_vertical > 0, below_val, above_val)
    advect_upwind = -DT_DX * (
        jnp.abs(velocity_horizontal) * (local_rows - up_x)
        + jnp.abs(velocity_vertical) * (local_rows - up_y)
    )
    state_delta = advect_upwind + relax[None, :, :, None] * (
        collision_term.astype(jnp.float32) - local_rows
    )
    retain_mask = (solid_own == 0)[None, :, :, None]
    return (local_rows + state_delta, retain_mask)


def on_device(dist, relax, flags, solid, inflow, basis, projection):
    velocity_horizontal, velocity_vertical, quadrature_weight = velocities(VX)
    table_first = mirror_table(VX, True)
    table_second = mirror_table(VX, False)
    cols = dist.shape[2]
    column_total = cols * lax.axis_size("space")
    first_column = lax.axis_index("space") * cols
    solid_all = jnp.pad(solid, ((0, 0), (1, 1)))
    padded_solid = lax.dynamic_slice_in_dim(solid_all, first_column, cols + 2, 1)

    def node_side(piece):
        node = jnp.einsum("qk,krcv->qrcv", basis, piece, preferred_element_type=jnp.float32)
        rho, mx, my, en = velocity_moments(
            node, velocity_horizontal, velocity_vertical, quadrature_weight
        )
        equil = maxwell(rho, mx, my, en, velocity_horizontal, velocity_vertical).astype(
            jnp.bfloat16
        )
        return jnp.einsum(
            "kq,qrcv->krcv", projection, equil, preferred_element_type=jnp.float32
        ).astype(jnp.bfloat16)

    def apply_collision(density_field):
        mapped = node_side(
            lax.all_to_all(density_field, "mode", split_axis=2, concat_axis=0, tiled=True)
        )
        return lax.all_to_all(mapped, "mode", split_axis=0, concat_axis=2, tiled=True)

    def run_section(density_field):
        padded_state = extended(density_field, (("space", 2),), 1)
        collision_term = apply_collision(density_field)
        return heun_update(
            padded_state,
            collision_term,
            relax,
            flags,
            padded_solid,
            inflow,
            first_column,
            column_total,
            velocity_horizontal,
            velocity_vertical,
            table_first,
            table_second,
        )

    after_step, retain_mask = run_section(dist)
    section = jnp.where(retain_mask, after_step, 0.0).astype(jnp.bfloat16)
    stepped_again, retain_mask = run_section(section)
    result = 0.5 * dist.astype(jnp.float32) + 0.5 * stepped_again
    return jnp.where(retain_mask, result, 0.0).astype(jnp.bfloat16)


def solution(mesh):
    placed = (
        P("mode", None, "space", None),
        P(None, "space"),
        P(None, "space"),
        P(),
        P("mode", None),
        P(),
        P(),
    )
    return jax.shard_map(
        on_device,
        mesh=mesh,
        in_specs=placed,
        out_specs=P("mode", None, "space", None),
        check_vma=False,
    )
```

profile of v0, /device:TPU:14, one launch (start us, length us, event | category | flops | bytes accessed | tf_op | source)
XLA Modules:
  0.0 102.9 jit_solution(7204015918817468213)
XLA Ops:
  0.0 2.2 %copy.125 = bf16[16,2,16,576]{3,0,1,2:T(8,128)(2,1)} copy(bf16[16,2,16,576]{3,2,1,0:T(8,128)(2,1)} %param.15) | data formatting | bytes 1179648 | tf_op args[0]
  2.2 6.3 %all-to-all-start = ((bf16[16,2,16,576]{3,0,1,2:T(8,128)(2,1)}), bf16[16,2,16,576]{3,0,1,2:T(8,128)(2,1)S(1)}, u32[]{:S(2)}, u32[]{:S(2)}) async-start(bf16[16,2,16,576]{3,0,1,2:T(8,128)(2,1)} %copy.125), calls=%async_computation | async-start | bytes 1310720 | tf_op jit(solution)/shard_map/all_to_all | solution.py:174
  8.8 7.6 %collective-permute-start.1 = (bf16[16,2,1,576]{3,0,2,1:T(8,128)(2,1)S(1)}, bf16[16,2,1,576]{3,0,2,1:T(8,128)(2,1)}, u32[]{:S(2)}, u32[]{:S(2)}) collective-permute-start(bf16[16,2,1,576]{3,0,2,1:T(8,128)(2,1)S(1)} %get-tuple-element.80), channel_id=1, source_target_pairs={{16,0},{32,16},{48,32},{64,48},{80,64},{96,80},{112,96},{128,112},... | collective-permute-start | bytes 110600 | tf_op jit(solution)/shard_map/ppermute | solution.py:27
  16.4 1.9 %collective-permute-start = (bf16[16,2,1,576]{3,0,2,1:T(8,128)(2,1)S(1)}, bf16[16,2,1,576]{3,0,2,1:T(8,128)(2,1)}, u32[]{:S(2)}, u32[]{:S(2)}) collective-permute-start(bf16[16,2,1,576]{3,0,2,1:T(8,128)(2,1)S(1)} %get-tuple-element.79), channel_id=1, source_target_pairs={{0,16},{16,32},{32,48},{48,64},{64,80},{80,96},{96,112},{112,128},... | collective-permute-start | bytes 110600 | tf_op jit(solution)/shard_map/ppermute | solution.py:25
  21.6 1.3 %slice_compare_fusion.2 = (pred[2,16]{1,0:T(4,128)(4,1)}, pred[2,16]{1,0:T(4,128)(4,1)S(1)}, pred[2,16]{1,0:T(4,128)(4,1)S(1)}, pred[2,16]{1,0:T(4,128)(4,1)}, pred[2,16]{1,0:T(4,128)(4,1)}) fusion(s32[2,18]{1,0:T(2,128)S(1)} %pad_dynamic-slice_fusion, s32[2,16]{1,0:T(2,128)} %param.17), kind=kLoop, calls=%fused_computation.150 | loop fusion | flops 160 | bytes 672 | tf_op jit(solution)/shard_map/eq | solution.py:146
  22.9 1.8 %fusion.53 = f32[16,2,2,576]{3,0,2,1:T(8,128)} fusion(s32[576]{0:T(1024)} %fusion.103, bf16[16,2,1,576]{3,0,2,1:T(8,128)(2,1)S(1)} %get-tuple-element.79, bf16[16,2,1,576]{3,0,2,1:T(8,128)(2,1)S(1)} %get-tuple-element.80, f32[16,576]{1,0:T(8,128)S(1)} %convert_element_type.164, pred[2,2]{1,0:T(4,128)(4,1)S(1)} %get-tuple-element.88, ...), kind=kOutput, calls=%fused_computation.67 | convolution fusion | flops 42983424 | bytes 260360 | tf_op jit(solution)/shard_map/krcv,vw->krcw/dot_general | solution.py:109
  28.0 1.8 %copy.128 = bf16[256,2,1,576]{3,1,2,0:T(2,128)(2,1)} copy(bf16[256,2,1,576]{0,3,1,2:T(8,128)(2,1)S(1)} %fusion.48) | data formatting | bytes 1179648 | tf_op jit(solution)/shard_map/convert_element_type | solution.py:170
  29.8 5.7 %all-to-all-start.1 = ((bf16[256,2,1,576]{3,1,2,0:T(2,128)(2,1)}), bf16[256,2,1,576]{3,1,2,0:T(2,128)(2,1)S(1)}, u32[]{:S(2)}, u32[]{:S(2)}) async-start(bf16[256,2,1,576]{3,1,2,0:T(2,128)(2,1)} %copy.128), calls=%async_computation.1 | async-start | bytes 1310720 | tf_op jit(solution)/shard_map/all_to_all | solution.py:176
  37.0 2.5 %convert_select_fusion.6 = (f32[16,2,16,576]{3,0,2,1:T(8,128)}, bf16[16,2,16,576]{3,0,2,1:T(8,128)(2,1)S(1)}) fusion(bf16[16,2,1,576]{3,0,2,1:T(8,128)(2,1)} %collective-permute-done.1, bf16[16,2,16,576]{3,0,2,1:T(8,128)(2,1)S(1)} %get-tuple-element.82, pred[2,16]{1,0:T(4,128)(4,1)S(1)} %get-tuple-element.90, bf16[16,2,16,640]{3,0,2,1:T(8,128)(2,1)S(1)} %reverse), kind=kLoop, calls=%fused_computation.6 | loop fusion | flops 1179648 | bytes 2986016 | tf_op jit(solution)/shard_map/jit(_where)/select_n | solution.py:118
  39.4 2.1 %convert_select_fusion.7 = f32[16,2,16,576]{3,0,2,1:T(8,128)} fusion(bf16[16,2,16,576]{3,0,2,1:T(8,128)(2,1)S(1)} %get-tuple-element.68, bf16[16,2,16,576]{3,0,2,1:T(8,128)(2,1)S(1)} %get-tuple-element.82, bf16[16,2,1,576]{3,0,2,1:T(8,128)(2,1)} %collective-permute-done, pred[2,16]{1,0:T(4,128)(4,1)S(1)} %get-tuple-element.91), kind=kLoop, calls=%fused_computation.7 | loop fusion | flops 1179648 | bytes 2396192 | tf_op jit(solution)/shard_map/jit(_where)/select_n | solution.py:117
  41.5 1.6 %fusion.87 = (f32[16,2,16,576]{3,0,2,1:T(8,128)}, f32[16,2,16,576]{3,0,2,1:T(8,128)}) fusion(f32[16,2,16,576]{3,0,2,1:T(8,128)} %get-tuple-element.67, f32[16,2,2,576]{3,0,2,1:T(8,128)S(1)} %copy-done.3, pred[]{:T(512)S(6)} %eq.127, f32[16,2,16,576]{3,0,2,1:T(8,128)} %convert_select_fusion.7, pred[]{:T(512)S(6)} %eq.120), kind=kLoop, calls=%fused_computation.100 | loop fusion | flops 36864 | bytes 475138 | tf_op jit(solution)/shard_map/scatter | solution.py:124
  43.2 1.9 %all-to-all-done.1 = bf16[256,2,1,576]{3,1,2,0:T(2,128)(2,1)S(1)} async-done(((bf16[256,2,1,576]{3,1,2,0:T(2,128)(2,1)}), bf16[256,2,1,576]{3,1,2,0:T(2,128)(2,1)S(1)}, u32[]{:S(2)}, u32[]{:S(2)}) %all-to-all-start.1) | async-done | bytes 589856 | tf_op jit(solution)/shard_map/all_to_all | solution.py:176
  46.6 4.0 %fusion.36 = bf16[16,2,16,576]{3,0,2,1:T(8,128)(2,1)S(1)} fusion(f32[16,2,16,576]{3,0,2,1:T(8,128)S(1)} %bitcast.94, bf16[16,2,16,576]{3,0,2,1:T(8,128)(2,1)S(1)} %get-tuple-element.68, f32[16,1,16,576]{3,0,2,1:T(8,128)} %get-tuple-element.74, f32[16,1,16,576]{3,0,2,1:T(8,128)} %get-tuple-element.73, f32[16,2,16,576]{3,0,2,1:T(8,128)} %get-tuple-element.86, ...), kind=kOutput, calls=%fused_computation.46 | convolution fusion | flops 346558464 | bytes 6533284 | tf_op jit(solution)/shard_map/krcv,vw->krcw/dot_general | solution.py:102
  51.5 6.1 %all-to-all-start.2 = ((bf16[16,2,16,576]{3,0,1,2:T(8,128)(2,1)}), bf16[16,2,16,576]{3,0,1,2:T(8,128)(2,1)S(1)}, u32[]{:S(2)}, u32[]{:S(2)}) async-start(bf16[16,2,16,576]{3,0,1,2:T(8,128)(2,1)} %copy.133), calls=%async_computation.2 | async-start | bytes 1310720 | tf_op jit(solution)/shard_map/all_to_all | solution.py:174
  58.8 8.5 %all-to-all-done.2 = bf16[16,2,16,576]{3,0,1,2:T(8,128)(2,1)S(1)} async-done(((bf16[16,2,16,576]{3,0,1,2:T(8,128)(2,1)}), bf16[16,2,16,576]{3,0,1,2:T(8,128)(2,1)S(1)}, u32[]{:S(2)}, u32[]{:S(2)}) %all-to-all-start.2) | async-done | bytes 589856 | tf_op jit(solution)/shard_map/all_to_all | solution.py:174
  68.6 1.8 %copy.136 = bf16[256,2,1,576]{3,1,2,0:T(2,128)(2,1)} copy(bf16[256,2,1,576]{0,3,1,2:T(8,128)(2,1)S(1)} %fusion.49) | data formatting | bytes 1179648 | tf_op jit(solution)/shard_map/convert_element_type | solution.py:170
  70.4 6.2 %all-to-all-start.3 = ((bf16[256,2,1,576]{3,1,2,0:T(2,128)(2,1)}), bf16[256,2,1,576]{3,1,2,0:T(2,128)(2,1)S(1)}, u32[]{:S(2)}, u32[]{:S(2)}) async-start(bf16[256,2,1,576]{3,1,2,0:T(2,128)(2,1)} %copy.136), calls=%async_computation.3 | async-start | bytes 1310720 | tf_op jit(solution)/shard_map/all_to_all | solution.py:176
  76.6 6.9 %collective-permute-start.3 = (bf16[16,2,1,576]{3,0,2,1:T(8,128)(2,1)S(1)}, bf16[16,2,1,576]{3,0,2,1:T(8,128)(2,1)}, u32[]{:S(2)}, u32[]{:S(2)}) collective-permute-start(bf16[16,2,1,576]{3,0,2,1:T(8,128)(2,1)S(1)} %get-tuple-element.76), channel_id=1, source_target_pairs={{16,0},{32,16},{48,32},{64,48},{80,64},{96,80},{112,96},{128,112},... | collective-permute-start | bytes 110600 | tf_op jit(solution)/shard_map/ppermute | solution.py:27
  83.6 2.1 %collective-permute-start.2 = (bf16[16,2,1,576]{3,0,2,1:T(8,128)(2,1)S(1)}, bf16[16,2,1,576]{3,0,2,1:T(8,128)(2,1)S(1)}, u32[]{:S(2)}, u32[]{:S(2)}) collective-permute-start(bf16[16,2,1,576]{3,0,2,1:T(8,128)(2,1)S(1)} %get-tuple-element.75), channel_id=1, source_target_pairs={{0,16},{16,32},{32,48},{48,64},{64,80},{80,96},{96,112},{112,128},... | collective-permute-start | bytes 110600 | tf_op jit(solution)/shard_map/ppermute | solution.py:25
  87.6 2.5 %convert_select_fusion.2 = (f32[16,2,16,576]{3,0,2,1:T(8,128)}, bf16[16,2,16,576]{3,0,2,1:T(8,128)(2,1)S(1)}) fusion(bf16[16,2,1,576]{3,0,2,1:T(8,128)(2,1)} %collective-permute-done.3, bf16[16,2,16,576]{3,0,2,1:T(8,128)(2,1)S(1)} %fusion.36, pred[2,16]{1,0:T(4,128)(4,1)S(1)} %get-tuple-element.90, bf16[16,2,16,640]{3,0,2,1:T(8,128)(2,1)S(1)} %reverse.1), kind=kLoop, calls=%fused_computation.2 | loop fusion | flops 1179648 | bytes 2986016 | tf_op jit(solution)/shard_map/jit(_where)/select_n | solution.py:118
  90.1 2.4 %collective-permute-done.2 = bf16[16,2,1,576]{3,0,2,1:T(8,128)(2,1)S(1)} collective-permute-done((bf16[16,2,1,576]{3,0,2,1:T(8,128)(2,1)S(1)}, bf16[16,2,1,576]{3,0,2,1:T(8,128)(2,1)S(1)}, u32[]{:S(2)}, u32[]{:S(2)}) %collective-permute-start.2) | collective-permute-done | bytes 36896 | tf_op jit(solution)/shard_map/ppermute | solution.py:25
  93.7 1.6 %fusion.85 = (f32[16,2,16,576]{3,0,2,1:T(8,128)}, f32[16,2,16,576]{3,0,2,1:T(8,128)}) fusion(f32[16,2,16,576]{3,0,2,1:T(8,128)} %get-tuple-element.61, f32[16,2,2,576]{3,0,2,1:T(8,128)S(1)} %copy-done.4, pred[]{:T(512)S(6)} %eq.127, f32[16,2,16,576]{3,0,2,1:T(8,128)} %convert_select_fusion.3, pred[]{:T(512)S(6)} %eq.120), kind=kLoop, calls=%fused_computation.96 | loop fusion | flops 36864 | bytes 475138 | tf_op jit(solution)/shard_map/scatter | solution.py:124
  96.6 1.3 %copy.138 = f32[256,2,1,576]{3,0,1,2:T(8,128)} copy(bf16[256,2,1,576]{0,3,2,1:T(8,128)(2,1)S(1)} %copy.137) | data formatting | bytes 1769472 | tf_op jit(solution)/shard_map/convert_element_type | solution.py:144
  98.0 4.0 %fusion.47 = bf16[16,2,16,576]{3,0,2,1:T(8,128)(2,1)S(1)} fusion(f32[16,2,16,576]{3,0,2,1:T(8,128)} %bitcast.93, f32[16,1,16,576]{3,0,2,1:T(8,128)} %get-tuple-element.78, f32[16,1,16,576]{3,0,2,1:T(8,128)S(1)} %copy-done.2, bf16[16,2,16,576]{3,0,2,1:T(8,128)(2,1)S(1)} %get-tuple-element.62, f32[16,2,16,576]{3,0,2,1:T(8,128)} %get-tuple-element.84, ...), kind=kOutput, calls=%fused_computation.55 | convolution fusion | flops 347443200 | bytes 7123108 | tf_op jit(solution)/shard_map/krcv,vw->krcw/dot_general | solution.py:102
  (124 shorter events, 18.2 us)
Async XLA Ops:
  0.0 27.4 %copy-start = (bf16[256,256]{1,0:T(8,128)(2,1)S(1)}, bf16[256,256]{1,0:T(8,128)(2,1)}, u32[]{:S(2)}) copy-start(bf16[256,256]{1,0:T(8,128)(2,1)} %param.21) | copy-start | bytes 393220
  0.0 8.5 %copy-start.1 = (bf16[16,2,16,576]{3,2,1,0:T(8,128)(2,1)S(1)}, bf16[16,2,16,576]{3,2,1,0:T(8,128)(2,1)}, u32[]{:S(2)}) copy-start(bf16[16,2,16,576]{3,2,1,0:T(8,128)(2,1)} %param.15) | copy-start | bytes 1769476
  2.2 23.7 %all-to-all-start = ((bf16[16,2,16,576]{3,0,1,2:T(8,128)(2,1)}), bf16[16,2,16,576]{3,0,1,2:T(8,128)(2,1)S(1)}, u32[]{:S(2)}, u32[]{:S(2)}) async-start(bf16[16,2,16,576]{3,0,1,2:T(8,128)(2,1)} %copy.125), calls=%async_computation | async-start | bytes 1310720 | tf_op jit(solution)/shard_map/all_to_all | solution.py:174
  8.5 12.2 %copy-start.6 = (s32[2,16]{1,0:T(2,128)S(1)}, s32[2,16]{1,0:T(2,128)}, u32[]{:S(2)}) copy-start(s32[2,16]{1,0:T(2,128)} %param.17) | copy-start | bytes 388
  8.5 12.3 %copy-start.14 = (s32[2,256]{1,0:T(2,128)S(1)}, s32[2,256]{1,0:T(2,128)}, u32[]{:S(2)}) copy-start(s32[2,256]{1,0:T(2,128)} %param.18) | copy-start | bytes 6148
  8.5 12.4 %copy-start.5 = (bf16[16,576]{1,0:T(8,128)(2,1)S(1)}, bf16[16,576]{1,0:T(8,128)(2,1)}, u32[]{:S(2)}) copy-start(bf16[16,576]{1,0:T(8,128)(2,1)} %param.19) | copy-start | bytes 55300
  8.8 28.1 %collective-permute-start.1 = (bf16[16,2,1,576]{3,0,2,1:T(8,128)(2,1)S(1)}, bf16[16,2,1,576]{3,0,2,1:T(8,128)(2,1)}, u32[]{:S(2)}, u32[]{:S(2)}) collective-permute-start(bf16[16,2,1,576]{3,0,2,1:T(8,128)(2,1)S(1)} %get-tuple-element.80), channel_id=1, source_target_pairs={{16,0},{32,16},{48,32},{64,48},{80,64},{96,80},{112,96},{128,112},... | collective-permute-start | bytes 110600 | tf_op jit(solution)/shard_map/ppermute | solution.py:27
  16.4 23.1 %collective-permute-start = (bf16[16,2,1,576]{3,0,2,1:T(8,128)(2,1)S(1)}, bf16[16,2,1,576]{3,0,2,1:T(8,128)(2,1)}, u32[]{:S(2)}, u32[]{:S(2)}) collective-permute-start(bf16[16,2,1,576]{3,0,2,1:T(8,128)(2,1)S(1)} %get-tuple-element.79), channel_id=1, source_target_pairs={{0,16},{16,32},{32,48},{48,64},{64,80},{80,96},{96,112},{112,128},... | collective-permute-start | bytes 110600 | tf_op jit(solution)/shard_map/ppermute | solution.py:25
  20.9 3.8 %copy-start.19 = (pred[2,2]{1,0:T(4,128)(4,1)}, pred[2,2]{1,0:T(4,128)(4,1)S(1)}, u32[]{:S(2)}) copy-start(pred[2,2]{1,0:T(4,128)(4,1)S(1)} %get-tuple-element.87) | copy-start | bytes 16
  20.9 3.8 %copy-start.21 = (pred[2,2]{1,0:T(4,128)(4,1)}, pred[2,2]{1,0:T(4,128)(4,1)S(1)}, u32[]{:S(2)}) copy-start(pred[2,2]{1,0:T(4,128)(4,1)S(1)} %get-tuple-element.88) | copy-start | bytes 16
  29.8 15.4 %all-to-all-start.1 = ((bf16[256,2,1,576]{3,1,2,0:T(2,128)(2,1)}), bf16[256,2,1,576]{3,1,2,0:T(2,128)(2,1)S(1)}, u32[]{:S(2)}, u32[]{:S(2)}) async-start(bf16[256,2,1,576]{3,1,2,0:T(2,128)(2,1)} %copy.128), calls=%async_computation.1 | async-start | bytes 1310720 | tf_op jit(solution)/shard_map/all_to_all | solution.py:176
  43.2 3.3 %copy-start.27 = (pred[2,16]{1,0:T(4,128)(4,1)S(1)}, pred[2,16]{1,0:T(4,128)(4,1)}, u32[]{:S(2)}) copy-start(pred[2,16]{1,0:T(4,128)(4,1)} %get-tuple-element.89) | copy-start | bytes 100
  43.2 3.3 %copy-start.29 = (pred[2,16]{1,0:T(4,128)(4,1)S(1)}, pred[2,16]{1,0:T(4,128)(4,1)}, u32[]{:S(2)}) copy-start(pred[2,16]{1,0:T(4,128)(4,1)} %get-tuple-element.100) | copy-start | bytes 100
  51.5 15.8 %all-to-all-start.2 = ((bf16[16,2,16,576]{3,0,1,2:T(8,128)(2,1)}), bf16[16,2,16,576]{3,0,1,2:T(8,128)(2,1)S(1)}, u32[]{:S(2)}, u32[]{:S(2)}) async-start(bf16[16,2,16,576]{3,0,1,2:T(8,128)(2,1)} %copy.133), calls=%async_computation.2 | async-start | bytes 1310720 | tf_op jit(solution)/shard_map/all_to_all | solution.py:174
  58.8 8.6 %copy-start.9 = (f32[576]{0:T(1024)S(1)}, f32[576]{0:T(1024)}, u32[]{:S(2)}) copy-start(f32[576]{0:T(1024)} %multiply_add_fusion) | copy-start | bytes 6916
  58.8 8.6 %copy-start.11 = (f32[576]{0:T(1024)S(1)}, f32[576]{0:T(1024)}, u32[]{:S(2)}) copy-start(f32[576]{0:T(1024)} %get-tuple-element.102) | copy-start | bytes 6916
  58.8 8.6 %copy-start.13 = (f32[576]{0:T(1024)S(1)}, f32[576]{0:T(1024)}, u32[]{:S(2)}) copy-start(f32[576]{0:T(1024)} %get-tuple-element.103) | copy-start | bytes 6916
  58.8 8.6 %copy-start.34 = (bf16[256,256]{1,0:T(8,128)(2,1)S(1)}, bf16[256,256]{1,0:T(8,128)(2,1)}, u32[]{:S(2)}) copy-start(bf16[256,256]{1,0:T(8,128)(2,1)} %param.20) | copy-start | bytes 393220
  68.6 17.1 %copy-start.7 = (s32[576]{0:T(1024)S(1)}, s32[576]{0:T(1024)}, u32[]{:S(2)}) copy-start(s32[576]{0:T(1024)} %fusion.103) | copy-start | bytes 6916
  68.6 17.1 %copy-start.20 = (pred[2,2]{1,0:T(4,128)(4,1)S(1)}, pred[2,2]{1,0:T(4,128)(4,1)}, u32[]{:S(2)}) copy-start(pred[2,2]{1,0:T(4,128)(4,1)} %copy-done.19) | copy-start | bytes 16
  68.6 17.1 %copy-start.22 = (pred[2,2]{1,0:T(4,128)(4,1)S(1)}, pred[2,2]{1,0:T(4,128)(4,1)}, u32[]{:S(2)}) copy-start(pred[2,2]{1,0:T(4,128)(4,1)} %copy-done.21) | copy-start | bytes 16
  70.4 25.0 %all-to-all-start.3 = ((bf16[256,2,1,576]{3,1,2,0:T(2,128)(2,1)}), bf16[256,2,1,576]{3,1,2,0:T(2,128)(2,1)S(1)}, u32[]{:S(2)}, u32[]{:S(2)}) async-start(bf16[256,2,1,576]{3,1,2,0:T(2,128)(2,1)} %copy.136), calls=%async_computation.3 | async-start | bytes 1310720 | tf_op jit(solution)/shard_map/all_to_all | solution.py:176
  76.6 11.0 %collective-permute-start.3 = (bf16[16,2,1,576]{3,0,2,1:T(8,128)(2,1)S(1)}, bf16[16,2,1,576]{3,0,2,1:T(8,128)(2,1)}, u32[]{:S(2)}, u32[]{:S(2)}) collective-permute-start(bf16[16,2,1,576]{3,0,2,1:T(8,128)(2,1)S(1)} %get-tuple-element.76), channel_id=1, source_target_pairs={{16,0},{32,16},{48,32},{64,48},{80,64},{96,80},{112,96},{128,112},... | collective-permute-start | bytes 110600 | tf_op jit(solution)/shard_map/ppermute | solution.py:27
  83.6 8.9 %collective-permute-start.2 = (bf16[16,2,1,576]{3,0,2,1:T(8,128)(2,1)S(1)}, bf16[16,2,1,576]{3,0,2,1:T(8,128)(2,1)S(1)}, u32[]{:S(2)}, u32[]{:S(2)}) collective-permute-start(bf16[16,2,1,576]{3,0,2,1:T(8,128)(2,1)S(1)} %get-tuple-element.75), channel_id=1, source_target_pairs={{0,16},{16,32},{32,48},{48,64},{64,80},{80,96},{96,112},{112,128},... | collective-permute-start | bytes 110600 | tf_op jit(solution)/shard_map/ppermute | solution.py:25
  (25 other events, 59.5 us)
where the time goes:
time: 104 us; the launch traced here: 103 us
  starting transfers between devices  42.9 us (41%)
  other arithmetic  16.8 us (16%)
  local copies, waits for them, and re-layouts  16.5 us (16%)
  matrix products  13.3 us (13%)
  waiting for transfers between devices  12.8 us (12%)
    ppermute x2, starting transfers between devices, extended(): lax.ppermute(head, axis, [((i + 1) % count, i) for i in range(ends)])  14.5 us
    all_to_all x2, starting transfers between devices, apply_collision(): lax.all_to_all(density_field, 'mode', split_axis=2, concat_axis=0, tiled=...  12.4 us
    all_to_all x2, starting transfers between devices, apply_collision(): lax.all_to_all(mapped, 'mode', split_axis=0, concat_axis=2, tiled=True)  11.9 us
    all_to_all x2, waiting for transfers between devices, apply_collision(): lax.all_to_all(density_field, 'mode', split_axis=2, concat_axis=0, tiled=...  8.48 us
    dot_general x2, matrix products, heun_update(): jnp.einsum('krcv,vw->krcw', state_half, table_second, preferred_element_t...  8.01 us
    select_n x2, other arithmetic, heun_update(): right_val = jnp.where(solid_right, bounce, right)  4.94 us
    unnamed x85, local copies, waits for them, and re-layouts  4.75 us
    ppermute x2, starting transfers between devices, extended(): lax.ppermute(tail, axis, [(i, (i + 1) % count) for i in range(ends)])  4.02 us
  transfers between devices with their start and end apart: 8, of which 3 were waited for; matrix products, arithmetic and copies ran while one was open for 26% of the time, Pallas kernels for 0%

commit v1 on v0

v1 whole, which is shorter than its diff:
```python
import math

import numpy as np
import jax
import jax.numpy as jnp
from jax import lax
from jax.experimental import pallas as pl
from jax.experimental.pallas import tpu as pltpu
from jax.sharding import PartitionSpec as P

VX = 24
V = 576
ROWS = 2
COLS = 16
OWN = 32
MODES = 16
K = 256
VMAX = 4.6
DT_DX = 0.09
RHO_FLOOR = 0.3
TEMP_FLOOR = 0.2
STEP = 2.0 * VMAX / (VX - 1)
WEIGHT = STEP * STEP
HALF = 0.5 * STEP
LOG2E = math.log2(math.e)

HALO = 32
FAR = 36
BOUNCE = 40
MIRROR = 76
EDGE = 112
INFLOW = 116
SLOTS = 117

F32 = jnp.float32
BF16 = jnp.bfloat16
NT = (((1,), (1,)), ((), ()))
CHUNKS = tuple((128 * j, min(128, V - 128 * j)) for j in range(5))
LIMIT = 56 * 1024 * 1024


def tables():
    index = np.arange(V)
    a, b = index // VX, index % VX
    odd_a, odd_b = 2 * a - (VX - 1), 2 * b - (VX - 1)
    tri = (odd_a * odd_a - 1) // 8 + (odd_b * odd_b - 1) // 8
    weights = np.stack([np.ones(V), odd_a, odd_b, tri], 1)
    weights = np.repeat(weights, 32, axis=1)
    mirror = (a * VX + (VX - 1 - b))[:, None] == index[None, :]
    bounce = (V - 1 - index)[:, None] == index[None, :]
    rows = np.zeros((8, V), np.float32)
    rows[0] = DT_DX * np.abs(-VMAX + STEP * a)
    rows[1] = DT_DX * np.abs(-VMAX + STEP * b)
    rows[2] = (a >= VX // 2).astype(np.float32)
    rows[3] = (b >= VX // 2).astype(np.float32)
    return (
        jnp.asarray(weights.astype(np.float32), BF16),
        jnp.asarray(mirror.astype(np.float32), BF16),
        jnp.asarray(bounce.astype(np.float32), BF16),
        jnp.asarray(rows),
    )


def lanes(shape):
    return lax.broadcasted_iota(jnp.int32, shape, len(shape) - 1)


def pieces(value):
    hi = value.astype(BF16)
    rest = value - hi.astype(F32)
    mid = rest.astype(BF16)
    low = (rest - mid.astype(F32)).astype(BF16)
    return hi, mid, low


def edges_kernel(dist, relax, flags, cells, to_left, to_right, wide):
    for j, (at, n) in enumerate(CHUNKS):
        wide[j, :, :n] = dist[:, :, :, at : at + n].reshape(ROWS * COLS * MODES, n).astype(F32)

    def cell_chunk(cell, j):
        return wide[j, pl.ds(cell, MODES, stride=OWN), :]

    for cell in range(OWN):
        for j, (at, n) in enumerate(CHUNKS):
            cells[cell, :, at : at + n] = cell_chunk(cell, j)[:, :n].astype(BF16)
    lane = lanes((MODES, 128))
    for out, near, far, first in ((to_left, 0, 1, 0), (to_right, COLS - 1, COLS - 2, 2)):
        for r in range(ROWS):
            hi, mid, low = pieces(jnp.full((MODES, 128), relax[r, near], F32))
            flag = jnp.full((MODES, 128), flags[r, near], jnp.int32).astype(F32)
            extra = jnp.where(
                lane == 64,
                hi.astype(F32),
                jnp.where(
                    lane == 65,
                    mid.astype(F32),
                    jnp.where(lane == 66, low.astype(F32), jnp.where(lane == 67, flag, 0.0)),
                ),
            )
            for j in range(5):
                value = cell_chunk(r * COLS + near, j)
                if j == 4:
                    value = jnp.where(lane < 64, value, extra)
                out[r * 8 + j] = value.astype(BF16)
            for j in range(3):
                value = cell_chunk(r * COLS + far, first + j)
                if first + j == 4:
                    value = jnp.where(lane < 64, value, 0.0)
                out[r * 8 + 5 + j] = value.astype(BF16)


def mirrored(slots, held, cells, mirror, bounce):
    rows = cells * MODES
    turned = jnp.dot(held[:rows, :], mirror[...], preferred_element_type=F32)
    slots[MIRROR : MIRROR + cells] = turned.reshape(cells, MODES, V)
    for e, cell in enumerate((0, COLS - 1, COLS, 2 * COLS - 1)):
        held[rows + e * MODES : rows + (e + 1) * MODES, :] = turned[
            cell * MODES : (cell + 1) * MODES
        ].astype(BF16)
    back = jnp.dot(held[: rows + 64, :], bounce[...], preferred_element_type=F32)
    slots[BOUNCE : BOUNCE + cells] = back[:rows].reshape(cells, MODES, V)
    slots[EDGE : EDGE + 4] = back[rows:].reshape(4, MODES, V)


def advection(slots, rows, h, left, right, below, above):
    up_x = jnp.where(rows[2:3, :] > 0.5, left, right)
    up_y = jnp.where(rows[3:4, :] > 0.5, below, above)
    return rows[0:1, :] * (up_x - h) + rows[1:2, :] * (up_y - h)


def sources(r, c, column, flags, solid):
    own = r * COLS + c
    flag = flags[r, c]
    bounced = BOUNCE + own
    last = COLS * 16 - 1
    left = jnp.where(c == 0, HALO + r * 2, own - 1)
    right = jnp.where(c == COLS - 1, HALO + r * 2 + 1, own + 1)
    solid_left = solid[r, jnp.maximum(column - 1, 0)] == 1
    solid_right = solid[r, jnp.minimum(column + 1, last)] == 1

    def edge(turned):
        return jnp.where(flag == 0, own, jnp.where(flag == 1, INFLOW, turned))

    left = jnp.where(column == 0, edge(EDGE + r * 2), jnp.where(solid_left, bounced, left))
    right = jnp.where(
        column == last, edge(EDGE + r * 2 + 1), jnp.where(solid_right, bounced, right)
    )
    outside = edge(MIRROR + own)
    other = (1 - r) * COLS + c
    inside = jnp.where(solid[1 - r, column] == 1, bounced, other)
    below, above = (outside, inside) if r == 0 else (inside, outside)
    return left, right, below, above


def explicit_kernel(
    cells, from_left, from_right, inflow, relax, flags, solid, weights, mirror, bounce, rows,
    pay, base, slots, held, high, low,
):
    first = lax.axis_index("space") * COLS
    own = cells[...]
    slots[:OWN] = own.astype(F32)
    held[: OWN * MODES, :] = own.reshape(OWN * MODES, V)
    slots[INFLOW] = inflow[...].astype(F32)
    for side, ref, start in ((0, from_left, 2), (1, from_right, 0)):
        for r in range(ROWS):
            at_halo = HALO + r * 2 + side
            for j, (at, n) in enumerate(CHUNKS):
                value = ref[r * 8 + j][:, :n]
                slots[at_halo, :, at : at + n] = value.astype(F32)
                held[at_halo * MODES : (at_halo + 1) * MODES, at : at + n] = value
            for j in range(3):
                at, n = CHUNKS[start + j]
                slots[FAR + r * 2 + side, :, at : at + n] = ref[r * 8 + 5 + j][:, :n].astype(F32)
    mirrored(slots, held, 36, mirror, bounce)

    def own_cell(c, carry):
        for r in range(ROWS):
            cell = r * COLS + c
            column = first + c
            left, right, below, above = sources(r, c, column, flags, solid)
            h = slots[cell]
            moved = advection(
                slots, rows, h, slots[left], slots[right], slots[below], slots[above]
            )
            value = h - relax[r, c] * h + moved
            value = jnp.where(solid[r, column] == 0, value, 0.0)
            base[cell] = value
            hi = value.astype(BF16)
            at = pl.multiple_of(cell * MODES, MODES)
            high[pl.ds(at, MODES), :] = hi
            low[pl.ds(at, MODES), :] = (value - hi.astype(F32)).astype(BF16)
        return carry

    lax.fori_loop(0, COLS, own_cell, 0)
    for side, ref in ((0, from_left), (1, from_right)):
        for r in range(ROWS):
            cell = HALO + r * 2 + side
            column = jnp.clip(first - 1 if side == 0 else first + COLS, 1, COLS * 16 - 2)
            extra = ref[r * 8 + 4].astype(F32)
            rate = extra[:, 64:65] + extra[:, 65:66] + extra[:, 66:67]
            flag = extra[:, 67:68]
            h = slots[cell]
            edge = r * COLS + (0 if side == 0 else COLS - 1)
            far = FAR + r * 2 + side
            near_left, near_right = (far, edge) if side == 0 else (edge, far)
            bounced = BOUNCE + cell
            left = slots[jnp.where(solid[r, column - 1] == 1, bounced, near_left)]
            right = slots[jnp.where(solid[r, column + 1] == 1, bounced, near_right)]
            outside = jnp.where(
                flag < 0.5, h, jnp.where(flag < 1.5, slots[INFLOW], slots[MIRROR + cell])
            )
            inside = slots[
                jnp.where(solid[1 - r, column] == 1, bounced, HALO + (1 - r) * 2 + side)
            ]
            below, above = (outside, inside) if r == 0 else (inside, outside)
            value = h - rate * h + advection(slots, rows, h, left, right, below, above)
            base[cell] = jnp.where(solid[r, column] == 0, value, 0.0)

    place = lanes((MODES, 128)) % 32

    def fold(sums, cell_list):
        total = jnp.zeros((MODES, 128), F32)
        for i, cell in enumerate(cell_list):
            total += jnp.where(place == i, sums[cell * MODES : (cell + 1) * MODES], 0.0)
        return total

    sums = jnp.dot(held[: 36 * MODES, :], weights[...], preferred_element_type=F32)
    next_sums = jnp.dot(high[...], weights[...], preferred_element_type=F32) + jnp.dot(
        low[...], weights[...], preferred_element_type=F32
    )
    out = (
        fold(sums, range(OWN)),
        fold(next_sums, range(OWN)),
        fold(sums, range(HALO, HALO + 4)),
    )
    for d in range(16):
        for i in range(3):
            pay[d, :, 128 * i : 128 * (i + 1)] = out[i]


def exact_nt(value, table):
    total = None
    for piece in pieces(value):
        part = lax.dot_general(piece, table, NT, preferred_element_type=F32)
        total = part if total is None else total + part
    return total


def set_parameters(par, at, sums):
    s0, s1, s2, s3 = sums
    n = s0.shape[0]
    rho = WEIGHT * s0
    mx = (WEIGHT * HALF) * s1
    my = (WEIGHT * HALF) * s2
    en = (WEIGHT * HALF * HALF) * (4.0 * s3 + s0)
    safe = jnp.maximum(rho, RHO_FLOOR)
    ux = mx / safe
    uy = my / safe
    temp = jnp.maximum(en / safe - 0.5 * (ux * ux + uy * uy), TEMP_FLOOR)
    par[0, at : at + n] = ux
    par[1, at : at + n] = uy
    par[2, at : at + n] = (-0.5 * LOG2E) / temp
    par[3, at : at + n] = safe / (2.0 * math.pi * temp)


def factors(par, cell):
    ux = par[0, pl.ds(cell, 1), :]
    uy = par[1, pl.ds(cell, 1), :]
    rate = par[2, pl.ds(cell, 1), :]
    scale = par[3, pl.ds(cell, 1), :]
    speed = lax.broadcasted_iota(jnp.int32, (VX, K), 0).astype(F32) * STEP - VMAX
    dx = speed - ux
    dy = speed - uy
    return scale * jnp.exp2(dx * dx * rate), jnp.exp2(dy * dy * rate)


def project(along_x, along_y, equil, projection):
    for i in range(VX // 2):
        pair = jnp.concatenate(
            [along_x[2 * i : 2 * i + 1] * along_y, along_x[2 * i + 1 : 2 * i + 2] * along_y], 0
        )
        equil[48 * i : 48 * (i + 1), :] = pair.astype(BF16)
    out = lax.dot_general(projection, equil[...], NT, preferred_element_type=F32)
    return out.astype(BF16).astype(F32)


def collide_kernel(
    gathered, basis, projection, base, cells, from_left, from_right, inflow, relax, flags, solid,
    mirror, bounce, rows,
    out, slots, held, par, sums1, equil, wide,
):
    first = lax.axis_index("space") * COLS
    mode = lax.axis_index("mode") * MODES
    mine = projection[pl.ds(pl.multiple_of(mode, MODES), MODES), :]
    turned = gathered[...].T
    node = exact_nt(turned[:128], basis[...])
    halo_node = exact_nt(turned[256:384], basis[...])
    set_parameters(par, 0, [node[32 * i : 32 * i + 32] for i in range(4)])
    set_parameters(par, 32, [halo_node[32 * i : 32 * i + 8] for i in range(4)])
    slots[INFLOW] = inflow[...].astype(F32)

    odd = (2 * lax.broadcasted_iota(jnp.int32, (VX, K), 0) - (VX - 1)).astype(F32)
    tri = (odd * odd - 1.0) * 0.125

    def sums_of(value):
        return (
            jnp.sum(value, 0, keepdims=True),
            jnp.sum(value * odd, 0, keepdims=True),
            jnp.sum(value * tri, 0, keepdims=True),
        )

    def first_stage(c, carry):
        for r in range(ROWS):
            cell = r * COLS + c
            along_x, along_y = factors(par, cell)
            coll = project(along_x, along_y, equil.at[r], mine)
            fluid = solid[r, first + c] == 0
            rate = jnp.where(fluid, relax[r, c], 0.0)
            section = (base[cell] + rate * coll).astype(BF16)
            slots[cell] = section.astype(F32)
            held[pl.ds(pl.multiple_of(cell * MODES, MODES), MODES), :] = section
            x0, x1, x2 = sums_of(along_x)
            y0, y1, y2 = sums_of(along_y)
            y0, y1, y2 = rate * y0, rate * y1, rate * y2
            sums1[pl.ds(cell, 1), :] = x0 * y0
            sums1[pl.ds(32 + cell, 1), :] = x1 * y0
            sums1[pl.ds(64 + cell, 1), :] = x0 * y1
            sums1[pl.ds(96 + cell, 1), :] = x2 * y0 + x0 * y2
        return carry

    lax.fori_loop(0, COLS, first_stage, 0)
    for side, ref in ((0, from_left), (1, from_right)):
        for r in range(ROWS):
            cell = HALO + r * 2 + side
            column = jnp.clip(first - 1 if side == 0 else first + COLS, 0, COLS * 16 - 1)
            extra = ref[r * 8 + 4].astype(F32)
            rate = extra[:, 64:65] + extra[:, 65:66] + extra[:, 66:67]
            rate = jnp.where(solid[r, column] == 0, rate, 0.0)
            along_x, along_y = factors(par, cell)
            coll = project(along_x, along_y, equil.at[r], mine)
            slots[cell] = (base[cell] + rate * coll).astype(BF16).astype(F32)

    mirrored(slots, held, 32, mirror, bounce)
    mixed = turned[128:256] + exact_nt(sums1[...], projection[...])
    node = exact_nt(mixed, basis[...])
    set_parameters(par, 0, [node[32 * i : 32 * i + 32] for i in range(4)])

    def second_stage(c, carry):
        for r in range(ROWS):
            cell = r * COLS + c
            column = first + c
            along_x, along_y = factors(par, cell)
            coll = project(along_x, along_y, equil.at[r], mine)
            left, right, below, above = sources(r, c, column, flags, solid)
            h = slots[cell]
            moved = advection(
                slots, rows, h, slots[left], slots[right], slots[below], slots[above]
            )
            value = h + moved + relax[r, c] * (coll - h)
            value = 0.5 * cells[cell].astype(F32) + 0.5 * value
            value = jnp.where(solid[r, column] == 0, value, 0.0)
            for j, (at, n) in enumerate(CHUNKS):
                wide[j, pl.ds(cell, MODES, stride=OWN), :n] = value[:, at : at + n]
        return carry

    lax.fori_loop(0, COLS, second_stage, 0)
    for j, (at, n) in enumerate(CHUNKS):
        out[:, :, :, at : at + n] = (
            wide[j, :, :n].astype(BF16).reshape(MODES, ROWS, COLS, n)
        )


def on_device(dist, relax, flags, solid, inflow, basis, projection):
    weights, mirror, bounce, rows = tables()
    vmem = pl.BlockSpec(memory_space=pltpu.VMEM)
    smem = pl.BlockSpec(memory_space=pltpu.SMEM)
    params = pltpu.CompilerParams(vmem_limit_bytes=LIMIT)

    cells, to_left, to_right = pl.pallas_call(
        edges_kernel,
        out_shape=(
            jax.ShapeDtypeStruct((OWN, MODES, V), BF16),
            jax.ShapeDtypeStruct((16, MODES, 128), BF16),
            jax.ShapeDtypeStruct((16, MODES, 128), BF16),
        ),
        in_specs=[vmem, smem, smem],
        out_specs=(vmem, vmem, vmem),
        scratch_shapes=[pltpu.VMEM((5, OWN * MODES, 128), F32)],
        compiler_params=params,
    )(dist, relax, flags)
    count = lax.axis_size("space")
    from_left = lax.ppermute(to_right, "space", [(i, (i + 1) % count) for i in range(count)])
    from_right = lax.ppermute(to_left, "space", [((i + 1) % count, i) for i in range(count)])

    pay, base = pl.pallas_call(
        explicit_kernel,
        out_shape=(
            jax.ShapeDtypeStruct((16, MODES, 384), F32),
            jax.ShapeDtypeStruct((36, MODES, V), F32),
        ),
        in_specs=[vmem] * 4 + [smem] * 3 + [vmem] * 4,
        out_specs=(vmem, vmem),
        scratch_shapes=[
            pltpu.VMEM((SLOTS, MODES, V), F32),
            pltpu.VMEM((640, V), BF16),
            pltpu.VMEM((OWN * MODES, V), BF16),
            pltpu.VMEM((OWN * MODES, V), BF16),
        ],
        compiler_params=params,
    )(cells, from_left, from_right, inflow, relax, flags, solid, weights, mirror, bounce, rows)
    gathered = lax.all_to_all(pay, "mode", split_axis=0, concat_axis=0, tiled=True)
    gathered = gathered.reshape(K, 384)

    return pl.pallas_call(
        collide_kernel,
        out_shape=jax.ShapeDtypeStruct((MODES, ROWS, COLS, V), BF16),
        in_specs=[vmem] * 8 + [smem] * 3 + [vmem] * 3,
        out_specs=vmem,
        scratch_shapes=[
            pltpu.VMEM((SLOTS, MODES, V), F32),
            pltpu.VMEM((576, V), BF16),
            pltpu.VMEM((4, 40, K), F32),
            pltpu.VMEM((128, K), F32),
            pltpu.VMEM((2, V, K), BF16),
            pltpu.VMEM((5, OWN * MODES, 128), F32),
        ],
        compiler_params=params,
    )(
        gathered, basis, projection, base, cells, from_left, from_right, inflow,
        relax, flags, solid, mirror, bounce, rows,
    )


def solution(mesh):
    placed = (
        P("mode", None, "space", None),
        P(None, "space"),
        P(None, "space"),
        P(),
        P("mode", None),
        P(),
        P(),
    )
    return jax.shard_map(
        on_device,
        mesh=mesh,
        in_specs=placed,
        out_specs=P("mode", None, "space", None),
        check_vma=False,
    )
```

time: 104 us -> 53.4 us (0.51)
  the two profiles are of different devices: /device:TPU:14 before, /device:TPU:1 now
where the time goes in v1:
time: 53.4 us; the launch traced here: 53.2 us
  Pallas kernels  25.4 us (48%)
  blocking collectives  16.1 us (30%)
  starting transfers between devices  9.05 us (17%)
  waiting for transfers between devices  1.96 us (4%)
  local copies, waits for them, and re-layouts  0.63 us (1%)
    all_to_all x1, blocking collectives, on_device(): lax.all_to_all(pay, 'mode', split_axis=0, concat_axis=0, tiled=True)  16.1 us
    pallas_call x1, Pallas kernels, on_device(): pl.pallas_call(collide_kernel, out_shape=jax.ShapeDtypeStruct((MODES, ROW...  16 us
    pallas_call x1, Pallas kernels, on_device(): pl.pallas_call(explicit_kernel, out_shape=(jax.ShapeDtypeStruct((16, MODE...  6.38 us
    ppermute x1, starting transfers between devices, on_device(): lax.ppermute(to_left, 'space', [((i + 1) % count, i) for i in range(count)])  5.23 us
    ppermute x1, starting transfers between devices, on_device(): lax.ppermute(to_right, 'space', [(i, (i + 1) % count) for i in range(coun...  3.82 us
    pallas_call x1, Pallas kernels, on_device(): pl.pallas_call(edges_kernel, out_shape=(jax.ShapeDtypeStruct((OWN, MODES,...  2.98 us
    ppermute x1, waiting for transfers between devices, on_device(): lax.ppermute(to_right, 'space', [(i, (i + 1) % count) for i in range(coun...  1.96 us
  transfers between devices with their start and end apart: 2, of which 1 were waited for; matrix products, arithmetic and copies ran while one was open for 0% of the time, Pallas kernels for 0%

profile of v1, /device:TPU:1, one launch (start us, length us, event | category | flops | bytes accessed | tf_op | source)
XLA Modules:
  0.0 53.2 jit_solution(6085281698800989755)
XLA Ops:
  0.0 3.0 %shard_map.109 = (bf16[32,16,576]{2,1,0:T(8,128)(2,1)}, bf16[16,16,128]{2,1,0:T(8,128)(2,1)}, bf16[16,16,128]{2,1,0:T(8,128)(2,1)}) custom-call(bf16[16,2,16,576]{3,2,1,0:T(8,128)(2,1)} %dist.1, f32[2,16]{1,0:T(2,128)} %relax.5, s32[2,16]{1,0:T(2,128)} %flags.5), custom_call_target="tpu_custom_call" | custom-call | tf_op jit(solution)/shard_map/pallas_call | solution.py:379
  3.0 3.8 %collective-permute-start = (bf16[16,16,128]{2,1,0:T(8,128)(2,1)}, bf16[16,16,128]{2,1,0:T(8,128)(2,1)S(1)}, u32[]{:S(2)}, u32[]{:S(2)}) collective-permute-start(bf16[16,16,128]{2,1,0:T(8,128)(2,1)} %get-tuple-element.11), channel_id=1, source_target_pairs={{0,16},{16,32},{32,48},{48,64},{64,80},{80,96},{96,112},{112,128},... | collective-permute-start | bytes 196616 | tf_op jit(solution)/shard_map/ppermute | solution.py:392
  6.8 5.2 %collective-permute-start.1 = (bf16[16,16,128]{2,1,0:T(8,128)(2,1)}, bf16[16,16,128]{2,1,0:T(8,128)(2,1)S(1)}, u32[]{:S(2)}, u32[]{:S(2)}) collective-permute-start(bf16[16,16,128]{2,1,0:T(8,128)(2,1)} %get-tuple-element.12), channel_id=1, source_target_pairs={{16,0},{32,16},{48,32},{64,48},{80,64},{96,80},{112,96},{128,112},... | collective-permute-start | bytes 196616 | tf_op jit(solution)/shard_map/ppermute | solution.py:393
  12.0 2.0 %collective-permute-done.from_left = bf16[16,16,128]{2,1,0:T(8,128)(2,1)S(1)} collective-permute-done((bf16[16,16,128]{2,1,0:T(8,128)(2,1)}, bf16[16,16,128]{2,1,0:T(8,128)(2,1)S(1)}, u32[]{:S(2)}, u32[]{:S(2)}) %collective-permute-start) | collective-permute-done | bytes 65568 | tf_op jit(solution)/shard_map/ppermute | solution.py:392
  14.0 0.0 copy-start
  14.0 0.0 collective-permute-done.1.from_right
  14.0 0.0 copy-start.1
  14.0 0.6 %copy-done = bf16[16,16,128]{2,1,0:T(8,128)(2,1)} copy-done((bf16[16,16,128]{2,1,0:T(8,128)(2,1)}, bf16[16,16,128]{2,1,0:T(8,128)(2,1)S(1)}, u32[]{:S(2)}) %copy-start) | copy-done | bytes 65560
  14.6 0.0 copy-done.1
  14.6 6.4 %shard_map.110 = (f32[16,16,384]{2,1,0:T(8,128)}, f32[36,16,576]{2,1,0:T(8,128)}) custom-call(bf16[32,16,576]{2,1,0:T(8,128)(2,1)} %get-tuple-element.10.cells, bf16[16,16,128]{2,1,0:T(8,128)(2,1)} %copy-done, bf16[16,16,128]{2,1,0:T(8,128)(2,1)} %copy-done.1, bf16[16,576]{1,0:T(8,128)(2,1)} %inflow.3, f32[2,16]{1,0:T(2,128)} %relax.5, s32[2,16]{1,0:T(2,128)} %flags.5, ...), custom_call_target="tpu_custom_call" | custom-call | tf_op jit(solution)/shard_map/pallas_call | solution.py:395
  21.0 16.1 %all_to_all.5 = f32[16,16,384]{2,1,0:T(8,128)} all-to-all(f32[16,16,384]{2,1,0:T(8,128)} %get-tuple-element.13), channel_id=1, replica_groups=mesh['space'=16,'mode'=16] {'mode'}, dimensions={0} | all-to-all | bytes 786432 | tf_op jit(solution)/shard_map/all_to_all | solution.py:411
  37.1 16.0 %shard_map.111 = bf16[16,2,16,576]{3,2,1,0:T(8,128)(2,1)} custom-call(f32[256,384]{1,0:T(8,128)} %bitcast.1, bf16[256,256]{1,0:T(8,128)(2,1)} %basis.1, bf16[256,256]{1,0:T(8,128)(2,1)} %projection.1, f32[36,16,576]{2,1,0:T(8,128)} %get-tuple-element.14.base, bf16[32,16,576]{2,1,0:T(8,128)(2,1)} %get-tuple-element.10.cells, bf16[16,16,128]{2,1,0:T(8,128)(2,1)} %copy-done, ...), custom_call_target="tpu_custom_call" | custom-call | tf_op jit(solution)/shard_map/pallas_call | solution.py:414
Async XLA Ops:
  3.0 11.0 %collective-permute-start = (bf16[16,16,128]{2,1,0:T(8,128)(2,1)}, bf16[16,16,128]{2,1,0:T(8,128)(2,1)S(1)}, u32[]{:S(2)}, u32[]{:S(2)}) collective-permute-start(bf16[16,16,128]{2,1,0:T(8,128)(2,1)} %get-tuple-element.11), channel_id=1, source_target_pairs={{0,16},{16,32},{32,48},{48,64},{64,80},{80,96},{96,112},{112,128},... | collective-permute-start | bytes 196616 | tf_op jit(solution)/shard_map/ppermute | solution.py:392
  6.8 7.2 %collective-permute-start.1 = (bf16[16,16,128]{2,1,0:T(8,128)(2,1)}, bf16[16,16,128]{2,1,0:T(8,128)(2,1)S(1)}, u32[]{:S(2)}, u32[]{:S(2)}) collective-permute-start(bf16[16,16,128]{2,1,0:T(8,128)(2,1)} %get-tuple-element.12), channel_id=1, source_target_pairs={{16,0},{32,16},{48,32},{64,48},{80,64},{96,80},{112,96},{128,112},... | collective-permute-start | bytes 196616 | tf_op jit(solution)/shard_map/ppermute | solution.py:393
  14.0 0.6 %copy-start = (bf16[16,16,128]{2,1,0:T(8,128)(2,1)}, bf16[16,16,128]{2,1,0:T(8,128)(2,1)S(1)}, u32[]{:S(2)}) copy-start(bf16[16,16,128]{2,1,0:T(8,128)(2,1)S(1)} %collective-permute-done.from_left) | copy-start | bytes 196612
  14.0 0.6 %copy-start.1 = (bf16[16,16,128]{2,1,0:T(8,128)(2,1)}, bf16[16,16,128]{2,1,0:T(8,128)(2,1)S(1)}, u32[]{:S(2)}) copy-start(bf16[16,16,128]{2,1,0:T(8,128)(2,1)S(1)} %collective-permute-done.1.from_right) | copy-start | bytes 196612

commit v2 on v1

--- a/solution.py
+++ b/solution.py
@@ -46,8 +46,12 @@
     tri = (odd_a * odd_a - 1) // 8 + (odd_b * odd_b - 1) // 8
     weights = np.stack([np.ones(V), odd_a, odd_b, tri], 1)
     weights = np.repeat(weights, 32, axis=1)
-    mirror = (a * VX + (VX - 1 - b))[:, None] == index[None, :]
-    bounce = (V - 1 - index)[:, None] == index[None, :]
+    turned = a * VX + (VX - 1 - b)
+    swap = np.zeros((1152, 128), np.float32)
+    lane = np.arange(128)
+    swap[191 - lane, lane] = 1.0
+    for at, left, out in ((256, 0, 0), (512, 0, 128), (896, 128, 256)):
+        swap[at + turned[out + lane] - left, lane] = 1.0
     rows = np.zeros((8, V), np.float32)
     rows[0] = DT_DX * np.abs(-VMAX + STEP * a)
     rows[1] = DT_DX * np.abs(-VMAX + STEP * b)
@@ -55,8 +59,7 @@
     rows[3] = (b >= VX // 2).astype(np.float32)
     return (
         jnp.asarray(weights.astype(np.float32), BF16),
-        jnp.asarray(mirror.astype(np.float32), BF16),
-        jnp.asarray(bounce.astype(np.float32), BF16),
+        jnp.asarray(swap, BF16),
         jnp.asarray(rows),
     )
 
@@ -73,16 +76,17 @@
     return hi, mid, low
 
 
-def edges_kernel(dist, relax, flags, cells, to_left, to_right, wide):
+def cell_chunk(wide, cell, j):
+    return wide[j, pl.ds(cell, MODES, stride=OWN), :]
+
+
+def widen(dist, wide):
     for j, (at, n) in enumerate(CHUNKS):
         wide[j, :, :n] = dist[:, :, :, at : at + n].reshape(ROWS * COLS * MODES, n).astype(F32)
 
-    def cell_chunk(cell, j):
-        return wide[j, pl.ds(cell, MODES, stride=OWN), :]
-
-    for cell in range(OWN):
-        for j, (at, n) in enumerate(CHUNKS):
-            cells[cell, :, at : at + n] = cell_chunk(cell, j)[:, :n].astype(BF16)
+
+def edges_kernel(dist, relax, flags, to_left, to_right, wide):
+    widen(dist, wide)
     lane = lanes((MODES, 128))
     for out, near, far, first in ((to_left, 0, 1, 0), (to_right, COLS - 1, COLS - 2, 2)):
         for r in range(ROWS):
@@ -98,28 +102,45 @@
                 ),
             )
             for j in range(5):
-                value = cell_chunk(r * COLS + near, j)
+                value = cell_chunk(wide, r * COLS + near, j)
                 if j == 4:
                     value = jnp.where(lane < 64, value, extra)
                 out[r * 8 + j] = value.astype(BF16)
             for j in range(3):
-                value = cell_chunk(r * COLS + far, first + j)
+                value = cell_chunk(wide, r * COLS + far, first + j)
                 if first + j == 4:
                     value = jnp.where(lane < 64, value, 0.0)
                 out[r * 8 + 5 + j] = value.astype(BF16)
 
 
-def mirrored(slots, held, cells, mirror, bounce):
+def turn(held, count, swap):
+    parts = ((0, 256, 256, 128), (0, 384, 512, 128), (128, 256, 896, 128), (384, 192, 256, 128), (384, 192, 512, 64))
+    return permuted(held, count, swap, parts)
+
+
+def reverse(held, count, swap):
+    parts = ((384, 192, 0, 128), (256, 256, 0, 128), (128, 256, 0, 128), (0, 256, 0, 128), (0, 128, 128, 64))
+    return permuted(held, count, swap, parts)
+
+
+def permuted(held, count, swap, parts):
+    return [
+        jnp.dot(held[:count, lane : lane + n], swap[at : at + n, :width], preferred_element_type=F32)
+        for lane, n, at, width in parts
+    ]
+
+
+def mirrored(slots, held, cells, swap):
     rows = cells * MODES
-    turned = jnp.dot(held[:rows, :], mirror[...], preferred_element_type=F32)
-    slots[MIRROR : MIRROR + cells] = turned.reshape(cells, MODES, V)
-    for e, cell in enumerate((0, COLS - 1, COLS, 2 * COLS - 1)):
-        held[rows + e * MODES : rows + (e + 1) * MODES, :] = turned[
-            cell * MODES : (cell + 1) * MODES
-        ].astype(BF16)
-    back = jnp.dot(held[: rows + 64, :], bounce[...], preferred_element_type=F32)
-    slots[BOUNCE : BOUNCE + cells] = back[:rows].reshape(cells, MODES, V)
-    slots[EDGE : EDGE + 4] = back[rows:].reshape(4, MODES, V)
+    for (at, n), part in zip(CHUNKS, turn(held, rows, swap)):
+        slots[MIRROR : MIRROR + cells, :, at : at + n] = part.reshape(cells, MODES, n)
+        for e, cell in enumerate((0, COLS - 1, COLS, 2 * COLS - 1)):
+            held[rows + e * MODES : rows + (e + 1) * MODES, at : at + n] = part[
+                cell * MODES : (cell + 1) * MODES
+            ].astype(BF16)
+    for (at, n), part in zip(CHUNKS, reverse(held, rows + 64, swap)):
+        slots[BOUNCE : BOUNCE + cells, :, at : at + n] = part[:rows].reshape(cells, MODES, n)
+        slots[EDGE : EDGE + 4, :, at : at + n] = part[rows:].reshape(4, MODES, n)
 
 
 def advection(slots, rows, h, left, right, below, above):
@@ -152,26 +173,45 @@
     return left, right, below, above
 
 
+def fold(sums, count):
+    place = lanes((MODES, 128)) % 32
+    total = jnp.zeros((MODES, 128), F32)
+    for i in range(count):
+        total += jnp.where(place == i, sums[i * MODES : (i + 1) * MODES], 0.0)
+    return total
+
+
+def split(value, high, low, cell):
+    hi = value.astype(BF16)
+    at = pl.multiple_of(cell * MODES, MODES)
+    high[pl.ds(at, MODES), :] = hi
+    low[pl.ds(at, MODES), :] = (value - hi.astype(F32)).astype(BF16)
+
+
 def explicit_kernel(
-    cells, from_left, from_right, inflow, relax, flags, solid, weights, mirror, bounce, rows,
-    pay, base, slots, held, high, low,
+    dist, inflow, relax, flags, solid, weights, swap, rows,
+    cells, ends, base, sums, wide, slots, held, high, low,
 ):
     first = lax.axis_index("space") * COLS
-    own = cells[...]
-    slots[:OWN] = own.astype(F32)
-    held[: OWN * MODES, :] = own.reshape(OWN * MODES, V)
+    widen(dist, wide)
+
+    def gather(c, carry):
+        for r in range(ROWS):
+            cell = r * COLS + c
+            at_held = pl.multiple_of(cell * MODES, MODES)
+            for j, (at, n) in enumerate(CHUNKS):
+                value = cell_chunk(wide, cell, j)[:, :n]
+                slots[cell, :, at : at + n] = value
+                held[pl.ds(at_held, MODES), at : at + n] = value.astype(BF16)
+        return carry
+
+    lax.fori_loop(0, COLS, gather, 0, unroll=2)
+    cells[...] = held[: OWN * MODES, :].reshape(OWN, MODES, V)
+    for e, cell in enumerate((0, COLS - 1, COLS, 2 * COLS - 1)):
+        ends[e] = held[cell * MODES : (cell + 1) * MODES, :]
     slots[INFLOW] = inflow[...].astype(F32)
-    for side, ref, start in ((0, from_left, 2), (1, from_right, 0)):
-        for r in range(ROWS):
-            at_halo = HALO + r * 2 + side
-            for j, (at, n) in enumerate(CHUNKS):
-                value = ref[r * 8 + j][:, :n]
-                slots[at_halo, :, at : at + n] = value.astype(F32)
-                held[at_halo * MODES : (at_halo + 1) * MODES, at : at + n] = value
-            for j in range(3):
-                at, n = CHUNKS[start + j]
-                slots[FAR + r * 2 + side, :, at : at + n] = ref[r * 8 + 5 + j][:, :n].astype(F32)
-    mirrored(slots, held, 36, mirror, bounce)
+    slots[HALO : HALO + 4] = jnp.zeros((4, MODES, V), F32)
+    mirrored(slots, held, OWN, swap)
 
     def own_cell(c, carry):
         for r in range(ROWS):
@@ -185,54 +225,80 @@
             value = h - relax[r, c] * h + moved
             value = jnp.where(solid[r, column] == 0, value, 0.0)
             base[cell] = value
-            hi = value.astype(BF16)
-            at = pl.multiple_of(cell * MODES, MODES)
-            high[pl.ds(at, MODES), :] = hi
-            low[pl.ds(at, MODES), :] = (value - hi.astype(F32)).astype(BF16)
+            split(value, high, low, cell)
         return carry
 
-    lax.fori_loop(0, COLS, own_cell, 0)
+    lax.fori_loop(0, COLS, own_cell, 0, unroll=4)
+    sums[0] = fold(
+        jnp.dot(held[: OWN * MODES, :], weights[...], preferred_element_type=F32), OWN
+    )
+    sums[1] = fold(
+        jnp.dot(high[...], weights[...], preferred_element_type=F32)
+        + jnp.dot(low[...], weights[...], preferred_element_type=F32),
+        OWN,
+    )
+
+
+def halo_kernel(
+    ends, from_left, from_right, sums, inflow, solid, weights, swap, rows,
+    pay, edge, near, far, turned, back, held,
+):
+    first = lax.axis_index("space") * COLS
+    last = COLS * 16 - 1
+    for side, ref, start in ((0, from_left, 2), (1, from_right, 0)):
+        for r in range(ROWS):
+            i = r * 2 + side
+            for j, (at, n) in enumerate(CHUNKS):
+                value = ref[r * 8 + j][:, :n]
+                near[i, :, at : at + n] = value.astype(F32)
+                held[i * MODES : (i + 1) * MODES, at : at + n] = value
+            for j in range(3):
+                at, n = CHUNKS[start + j]
+                far[i, :, at : at + n] = ref[r * 8 + 5 + j][:, :n].astype(F32)
+    for (at, n), part in zip(CHUNKS, turn(held, 64, swap)):
+        turned[:, :, at : at + n] = part.reshape(4, MODES, n)
+    for (at, n), part in zip(CHUNKS, reverse(held, 64, swap)):
+        back[:, :, at : at + n] = part.reshape(4, MODES, n)
+    source = inflow[...].astype(F32)
     for side, ref in ((0, from_left), (1, from_right)):
         for r in range(ROWS):
-            cell = HALO + r * 2 + side
-            column = jnp.clip(first - 1 if side == 0 else first + COLS, 1, COLS * 16 - 2)
+            i = r * 2 + side
+            beyond = first - 1 if side == 0 else first + COLS
+            column = jnp.clip(beyond, 1, last - 1)
             extra = ref[r * 8 + 4].astype(F32)
             rate = extra[:, 64:65] + extra[:, 65:66] + extra[:, 66:67]
             flag = extra[:, 67:68]
-            h = slots[cell]
-            edge = r * COLS + (0 if side == 0 else COLS - 1)
-            far = FAR + r * 2 + side
-            near_left, near_right = (far, edge) if side == 0 else (edge, far)
-            bounced = BOUNCE + cell
-            left = slots[jnp.where(solid[r, column - 1] == 1, bounced, near_left)]
-            right = slots[jnp.where(solid[r, column + 1] == 1, bounced, near_right)]
-            outside = jnp.where(
-                flag < 0.5, h, jnp.where(flag < 1.5, slots[INFLOW], slots[MIRROR + cell])
-            )
-            inside = slots[
-                jnp.where(solid[1 - r, column] == 1, bounced, HALO + (1 - r) * 2 + side)
-            ]
+            h = near[i]
+            own = ends[i].astype(F32)
+            bounced = back[i]
+            left, right = (far[i], own) if side == 0 else (own, far[i])
+            left = jnp.where(solid[r, column - 1] == 1, bounced, left)
+            right = jnp.where(solid[r, column + 1] == 1, bounced, right)
+            outside = jnp.where(flag < 0.5, h, jnp.where(flag < 1.5, source, turned[i]))
+            inside = jnp.where(solid[1 - r, column] == 1, bounced, near[(1 - r) * 2 + side])
             below, above = (outside, inside) if r == 0 else (inside, outside)
-            value = h - rate * h + advection(slots, rows, h, left, right, below, above)
-            base[cell] = jnp.where(solid[r, column] == 0, value, 0.0)
-
+            value = h - rate * h + advection(None, rows, h, left, right, below, above)
+            edge[4 + i] = jnp.where(solid[r, column] == 0, value, 0.0)
+
+            inner = first if side == 0 else first + COLS - 1
+            inside_band = (beyond >= 0) & (beyond <= last)
+            used = inside_band & (solid[r, jnp.clip(beyond, 0, last)] == 0) & (solid[r, inner] == 0)
+            taken = rows[2:3, :] > 0.5 if side == 0 else rows[2:3, :] < 0.5
+            value = jnp.where(taken, rows[0:1, :] * h, 0.0)
+            value = jnp.where(used, value, 0.0)
+            edge[i] = value
+            hi = value.astype(BF16)
+            held[64 + i * MODES : 80 + i * MODES, :] = hi
+            held[128 + i * MODES : 144 + i * MODES, :] = (value - hi.astype(F32)).astype(BF16)
+    edge[8] = jnp.zeros((MODES, V), F32)
+    folded = jnp.dot(held[...], weights[...], preferred_element_type=F32)
     place = lanes((MODES, 128)) % 32
-
-    def fold(sums, cell_list):
-        total = jnp.zeros((MODES, 128), F32)
-        for i, cell in enumerate(cell_list):
-            total += jnp.where(place == i, sums[cell * MODES : (cell + 1) * MODES], 0.0)
-        return total
-
-    sums = jnp.dot(held[: 36 * MODES, :], weights[...], preferred_element_type=F32)
-    next_sums = jnp.dot(high[...], weights[...], preferred_element_type=F32) + jnp.dot(
-        low[...], weights[...], preferred_element_type=F32
-    )
-    out = (
-        fold(sums, range(OWN)),
-        fold(next_sums, range(OWN)),
-        fold(sums, range(HALO, HALO + 4)),
-    )
+    added = folded[64:128] + folded[128:]
+    later = sums[1]
+    for i in range(4):
+        cell = (i // 2) * COLS + (0 if i % 2 == 0 else COLS - 1)
+        later += jnp.where(place == cell, added[i * MODES : (i + 1) * MODES], 0.0)
+    out = (sums[0], later, fold(folded, 4))
     for d in range(16):
         for i in range(3):
             pay[d, :, 128 * i : 128 * (i + 1)] = out[i]
@@ -285,10 +351,18 @@
 
 
 def collide_kernel(
-    gathered, basis, projection, base, cells, from_left, from_right, inflow, relax, flags, solid,
-    mirror, bounce, rows,
-    out, slots, held, par, sums1, equil, wide,
+    gathered, basis, projection, base_far, edge_far, cells_far, from_left, from_right, inflow,
+    relax, flags, solid, swap_far, rows,
+    out, slots, held, par, sums1, equil, wide, base, edge, cells, swap, arrived,
 ):
+    copies = [
+        pltpu.make_async_copy(source, target, arrived.at[i])
+        for i, (source, target) in enumerate(
+            ((base_far, base), (edge_far, edge), (cells_far, cells), (swap_far, swap))
+        )
+    ]
+    for copy in copies:
+        copy.start()
     first = lax.axis_index("space") * COLS
     mode = lax.axis_index("mode") * MODES
     mine = projection[pl.ds(pl.multiple_of(mode, MODES), MODES), :]
@@ -316,7 +390,8 @@
             coll = project(along_x, along_y, equil.at[r], mine)
             fluid = solid[r, first + c] == 0
             rate = jnp.where(fluid, relax[r, c], 0.0)
-            section = (base[cell] + rate * coll).astype(BF16)
+            end = jnp.where(c == 0, r * 2, jnp.where(c == COLS - 1, r * 2 + 1, 8))
+            section = (base[cell] + edge[end] + rate * coll).astype(BF16)
             slots[cell] = section.astype(F32)
             held[pl.ds(pl.multiple_of(cell * MODES, MODES), MODES), :] = section
             x0, x1, x2 = sums_of(along_x)
@@ -328,7 +403,9 @@
             sums1[pl.ds(96 + cell, 1), :] = x2 * y0 + x0 * y2
         return carry
 
-    lax.fori_loop(0, COLS, first_stage, 0)
+    for copy in copies:
+        copy.wait()
+    lax.fori_loop(0, COLS, first_stage, 0, unroll=4)
     for side, ref in ((0, from_left), (1, from_right)):
         for r in range(ROWS):
             cell = HALO + r * 2 + side
@@ -338,9 +415,9 @@
             rate = jnp.where(solid[r, column] == 0, rate, 0.0)
             along_x, along_y = factors(par, cell)
             coll = project(along_x, along_y, equil.at[r], mine)
-            slots[cell] = (base[cell] + rate * coll).astype(BF16).astype(F32)
-
-    mirrored(slots, held, 32, mirror, bounce)
+            slots[cell] = (edge[4 + r * 2 + side] + rate * coll).astype(BF16).astype(F32)
+
+    mirrored(slots, held, OWN, swap)
     mixed = turned[128:256] + exact_nt(sums1[...], projection[...])
     node = exact_nt(mixed, basis[...])
     set_parameters(par, 0, [node[32 * i : 32 * i + 32] for i in range(4)])
@@ -363,7 +440,7 @@
                 wide[j, pl.ds(cell, MODES, stride=OWN), :n] = value[:, at : at + n]
         return carry
 
-    lax.fori_loop(0, COLS, second_stage, 0)
+    lax.fori_loop(0, COLS, second_stage, 0, unroll=4)
     for j, (at, n) in enumerate(CHUNKS):
         out[:, :, :, at : at + n] = (
             wide[j, :, :n].astype(BF16).reshape(MODES, ROWS, COLS, n)
@@ -371,20 +448,20 @@
 
 
 def on_device(dist, relax, flags, solid, inflow, basis, projection):
-    weights, mirror, bounce, rows = tables()
+    weights, swap, rows = tables()
     vmem = pl.BlockSpec(memory_space=pltpu.VMEM)
     smem = pl.BlockSpec(memory_space=pltpu.SMEM)
+    far = pl.BlockSpec(memory_space=pl.ANY)
     params = pltpu.CompilerParams(vmem_limit_bytes=LIMIT)
 
-    cells, to_left, to_right = pl.pallas_call(
+    to_left, to_right = pl.pallas_call(
         edges_kernel,
         out_shape=(
-            jax.ShapeDtypeStruct((OWN, MODES, V), BF16),
             jax.ShapeDtypeStruct((16, MODES, 128), BF16),
             jax.ShapeDtypeStruct((16, MODES, 128), BF16),
         ),
         in_specs=[vmem, smem, smem],
-        out_specs=(vmem, vmem, vmem),
+        out_specs=(vmem, vmem),
         scratch_shapes=[pltpu.VMEM((5, OWN * MODES, 128), F32)],
         compiler_params=params,
     )(dist, relax, flags)
@@ -392,29 +469,47 @@
     from_left = lax.ppermute(to_right, "space", [(i, (i + 1) % count) for i in range(count)])
     from_right = lax.ppermute(to_left, "space", [((i + 1) % count, i) for i in range(count)])
 
-    pay, base = pl.pallas_call(
+    cells, ends, base, sums = pl.pallas_call(
         explicit_kernel,
         out_shape=(
-            jax.ShapeDtypeStruct((16, MODES, 384), F32),
-            jax.ShapeDtypeStruct((36, MODES, V), F32),
+            jax.ShapeDtypeStruct((OWN, MODES, V), BF16),
+            jax.ShapeDtypeStruct((4, MODES, V), BF16),
+            jax.ShapeDtypeStruct((OWN, MODES, V), F32),
+            jax.ShapeDtypeStruct((2, MODES, 128), F32),
         ),
-        in_specs=[vmem] * 4 + [smem] * 3 + [vmem] * 4,
-        out_specs=(vmem, vmem),
+        in_specs=[vmem] * 2 + [smem] * 3 + [vmem] * 3,
+        out_specs=(vmem, vmem, vmem, vmem),
         scratch_shapes=[
+            pltpu.VMEM((5, OWN * MODES, 128), F32),
             pltpu.VMEM((SLOTS, MODES, V), F32),
-            pltpu.VMEM((640, V), BF16),
+            pltpu.VMEM((576, V), BF16),
             pltpu.VMEM((OWN * MODES, V), BF16),
             pltpu.VMEM((OWN * MODES, V), BF16),
         ],
         compiler_params=params,
-    )(cells, from_left, from_right, inflow, relax, flags, solid, weights, mirror, bounce, rows)
+        cost_estimate=pl.CostEstimate(
+            flops=20_000_000_000, bytes_accessed=4_000_000, transcendentals=0
+        ),
+    )(dist, inflow, relax, flags, solid, weights, swap, rows)
+
+    pay, edge = pl.pallas_call(
+        halo_kernel,
+        out_shape=(
+            jax.ShapeDtypeStruct((16, MODES, 384), F32),
+            jax.ShapeDtypeStruct((9, MODES, V), F32),
+        ),
+        in_specs=[vmem] * 5 + [smem] + [vmem] * 3,
+        out_specs=(vmem, vmem),
+        scratch_shapes=[pltpu.VMEM((4, MODES, V), F32)] * 4 + [pltpu.VMEM((192, V), BF16)],
+        compiler_params=params,
+    )(ends, from_left, from_right, sums, inflow, solid, weights, swap, rows)
     gathered = lax.all_to_all(pay, "mode", split_axis=0, concat_axis=0, tiled=True)
     gathered = gathered.reshape(K, 384)
 
     return pl.pallas_call(
         collide_kernel,
         out_shape=jax.ShapeDtypeStruct((MODES, ROWS, COLS, V), BF16),
-        in_specs=[vmem] * 8 + [smem] * 3 + [vmem] * 3,
+        in_specs=[vmem] * 3 + [far] * 3 + [vmem] * 3 + [smem] * 3 + [far, vmem],
         out_specs=vmem,
         scratch_shapes=[
             pltpu.VMEM((SLOTS, MODES, V), F32),
@@ -423,11 +518,16 @@
             pltpu.VMEM((128, K), F32),
             pltpu.VMEM((2, V, K), BF16),
             pltpu.VMEM((5, OWN * MODES, 128), F32),
+            pltpu.VMEM((OWN, MODES, V), F32),
+            pltpu.VMEM((9, MODES, V), F32),
+            pltpu.VMEM((OWN, MODES, V), BF16),
+            pltpu.VMEM((1152, 128), BF16),
+            pltpu.SemaphoreType.DMA((4,)),
         ],
         compiler_params=params,
     )(
-        gathered, basis, projection, base, cells, from_left, from_right, inflow,
-        relax, flags, solid, mirror, bounce, rows,
+        gathered, basis, projection, base, edge, cells, from_left, from_right, inflow,
+        relax, flags, solid, swap, rows,
     )
 
 

time: 53.4 us -> 47.4 us (0.89)
  Pallas kernels: 25.4 us -> 23 us
  waiting for transfers between devices: 1.96 us -> 0.01 us
  blocking collectives: 16.1 us -> 14.4 us
    pallas_call x1, Pallas kernels: 16 us -> 12.8 us  [on_device(): pl.pallas_call(collide_kernel, out_shape=jax.ShapeDtypeStruct((MODES, ROW...]
    ppermute x1, waiting for transfers between devices: 1.96 us -> 0.01 us  [on_device(): lax.ppermute(to_right, 'space', [(i, (i + 1) % count) for i in range(coun...]
    all_to_all x1, blocking collectives: 16.1 us -> 14.4 us  [on_device(): lax.all_to_all(pay, 'mode', split_axis=0, concat_axis=0, tiled=True)]
    pallas_call x2 -> x3, Pallas kernels: 9.36 us -> 10.2 us  [the longest x1 5.79 us: on_device(): pl.pallas_call(explicit_kernel, out_shape=(jax.ShapeDtypeStruct((OWN, MOD...]
  transfers between devices with their start and end apart: 2 -> 2, of which waited for: 1 -> 0; matrix products, arithmetic and copies ran while one was open for 0% -> 0% of each run, Pallas kernels for 0% -> 12%
where the time goes in v2:
time: 47.4 us; the launch traced here: 47.1 us
  Pallas kernels  23 us (49%)
  blocking collectives  14.4 us (30%)
  starting transfers between devices  9.05 us (19%)
  local copies, waits for them, and re-layouts  0.62 us (1%)
    all_to_all x1, blocking collectives, on_device(): lax.all_to_all(pay, 'mode', split_axis=0, concat_axis=0, tiled=True)  14.4 us
    pallas_call x1, Pallas kernels, on_device(): pl.pallas_call(collide_kernel, out_shape=jax.ShapeDtypeStruct((MODES, ROW...  12.8 us
    pallas_call x1, Pallas kernels, on_device(): pl.pallas_call(explicit_kernel, out_shape=(jax.ShapeDtypeStruct((OWN, MOD...  5.79 us
    ppermute x1, starting transfers between devices, on_device(): lax.ppermute(to_left, 'space', [((i + 1) % count, i) for i in range(count)])  5.23 us
    ppermute x1, starting transfers between devices, on_device(): lax.ppermute(to_right, 'space', [(i, (i + 1) % count) for i in range(coun...  3.82 us
    pallas_call x1, Pallas kernels, on_device(): pl.pallas_call(halo_kernel, out_shape=(jax.ShapeDtypeStruct((16, MODES, 3...  2.42 us
    pallas_call x1, Pallas kernels, on_device(): pl.pallas_call(edges_kernel, out_shape=(jax.ShapeDtypeStruct((16, MODES,...  1.97 us
  transfers between devices with their start and end apart: 2, of which 0 were waited for; matrix products, arithmetic and copies ran while one was open for 0% of the time, Pallas kernels for 12%

profile of v2, /device:TPU:1, one launch (start us, length us, event | category | flops | bytes accessed | tf_op | source)
XLA Modules:
  0.0 47.1 jit_solution(215044544386658508)
XLA Ops:
  0.0 2.0 %shard_map.101 = (bf16[16,16,128]{2,1,0:T(8,128)(2,1)}, bf16[16,16,128]{2,1,0:T(8,128)(2,1)}) custom-call(bf16[16,2,16,576]{3,2,1,0:T(8,128)(2,1)} %dist.3, f32[2,16]{1,0:T(2,128)} %relax.5, s32[2,16]{1,0:T(2,128)} %flags.5), custom_call_target="tpu_custom_call" | custom-call | tf_op jit(solution)/shard_map/pallas_call | solution.py:457
  2.0 3.8 %collective-permute-start = (bf16[16,16,128]{2,1,0:T(8,128)(2,1)}, bf16[16,16,128]{2,1,0:T(8,128)(2,1)S(1)}, u32[]{:S(2)}, u32[]{:S(2)}) collective-permute-start(bf16[16,16,128]{2,1,0:T(8,128)(2,1)} %get-tuple-element.14), channel_id=1, source_target_pairs={{0,16},{16,32},{32,48},{48,64},{64,80},{80,96},{96,112},{112,128},... | collective-permute-start | bytes 196616 | tf_op jit(solution)/shard_map/ppermute | solution.py:469
  5.8 5.2 %collective-permute-start.1 = (bf16[16,16,128]{2,1,0:T(8,128)(2,1)}, bf16[16,16,128]{2,1,0:T(8,128)(2,1)S(1)}, u32[]{:S(2)}, u32[]{:S(2)}) collective-permute-start(bf16[16,16,128]{2,1,0:T(8,128)(2,1)} %get-tuple-element.15), channel_id=1, source_target_pairs={{16,0},{32,16},{48,32},{64,48},{80,64},{96,80},{112,96},{128,112},... | collective-permute-start | bytes 196616 | tf_op jit(solution)/shard_map/ppermute | solution.py:470
  11.0 5.8 %shard_map.100 = (bf16[32,16,576]{2,1,0:T(8,128)(2,1)}, bf16[4,16,576]{2,1,0:T(8,128)(2,1)}, f32[32,16,576]{2,1,0:T(8,128)}, f32[2,16,128]{2,1,0:T(8,128)}) custom-call(bf16[16,2,16,576]{3,2,1,0:T(8,128)(2,1)} %dist.3, bf16[16,576]{1,0:T(8,128)(2,1)} %inflow.5, f32[2,16]{1,0:T(2,128)} %relax.5, s32[2,16]{1,0:T(2,128)} %flags.5, s32[2,256]{1,0:T(2,128)} %solid.5, ...), custom_call_target="tpu_custom_call" | custom-call | flops 20000000000 | bytes 4000000 | tf_op jit(solution)/shard_map/pallas_call | solution.py:472
  16.8 0.0 collective-permute-done.from_left
  16.8 0.0 copy-start
  16.8 0.0 collective-permute-done.1.from_right
  16.8 0.0 copy-start.1
  16.8 0.6 %copy-done = bf16[16,16,128]{2,1,0:T(8,128)(2,1)} copy-done((bf16[16,16,128]{2,1,0:T(8,128)(2,1)}, bf16[16,16,128]{2,1,0:T(8,128)(2,1)S(1)}, u32[]{:S(2)}) %copy-start) | copy-done | bytes 65560
  17.4 0.0 copy-done.1
  17.5 2.4 %shard_map.102 = (f32[16,16,384]{2,1,0:T(8,128)}, f32[9,16,576]{2,1,0:T(8,128)}) custom-call(bf16[4,16,576]{2,1,0:T(8,128)(2,1)} %get-tuple-element.13.ends, bf16[16,16,128]{2,1,0:T(8,128)(2,1)} %copy-done, bf16[16,16,128]{2,1,0:T(8,128)(2,1)} %copy-done.1, f32[2,16,128]{2,1,0:T(8,128)} %get-tuple-element.16.sums, bf16[16,576]{1,0:T(8,128)(2,1)} %inflow.5, ...), custom_call_target="tpu_custom_call" | custom-call | tf_op jit(solution)/shard_map/pallas_call | solution.py:495
  19.9 14.4 %all_to_all.5 = f32[16,16,384]{2,1,0:T(8,128)} all-to-all(f32[16,16,384]{2,1,0:T(8,128)} %get-tuple-element.17), channel_id=1, replica_groups=mesh['space'=16,'mode'=16] {'mode'}, dimensions={0} | all-to-all | bytes 786432 | tf_op jit(solution)/shard_map/all_to_all | solution.py:506
  34.3 12.8 %shard_map.103 = bf16[16,2,16,576]{3,2,1,0:T(8,128)(2,1)} custom-call(f32[256,384]{1,0:T(8,128)} %bitcast.1, bf16[256,256]{1,0:T(8,128)(2,1)} %basis.1, bf16[256,256]{1,0:T(8,128)(2,1)} %projection.1, f32[32,16,576]{2,1,0:T(8,128)} %get-tuple-element.18.base_far, f32[9,16,576]{2,1,0:T(8,128)} %get-tuple-element.19.edge_far, ...), custom_call_target="tpu_custom_call" | custom-call | tf_op jit(solution)/shard_map/pallas_call | solution.py:509
Async XLA Ops:
  2.0 14.8 %collective-permute-start = (bf16[16,16,128]{2,1,0:T(8,128)(2,1)}, bf16[16,16,128]{2,1,0:T(8,128)(2,1)S(1)}, u32[]{:S(2)}, u32[]{:S(2)}) collective-permute-start(bf16[16,16,128]{2,1,0:T(8,128)(2,1)} %get-tuple-element.14), channel_id=1, source_target_pairs={{0,16},{16,32},{32,48},{48,64},{64,80},{80,96},{96,112},{112,128},... | collective-permute-start | bytes 196616 | tf_op jit(solution)/shard_map/ppermute | solution.py:469
  5.8 11.0 %collective-permute-start.1 = (bf16[16,16,128]{2,1,0:T(8,128)(2,1)}, bf16[16,16,128]{2,1,0:T(8,128)(2,1)S(1)}, u32[]{:S(2)}, u32[]{:S(2)}) collective-permute-start(bf16[16,16,128]{2,1,0:T(8,128)(2,1)} %get-tuple-element.15), channel_id=1, source_target_pairs={{16,0},{32,16},{48,32},{64,48},{80,64},{96,80},{112,96},{128,112},... | collective-permute-start | bytes 196616 | tf_op jit(solution)/shard_map/ppermute | solution.py:470
  16.8 0.6 %copy-start = (bf16[16,16,128]{2,1,0:T(8,128)(2,1)}, bf16[16,16,128]{2,1,0:T(8,128)(2,1)S(1)}, u32[]{:S(2)}) copy-start(bf16[16,16,128]{2,1,0:T(8,128)(2,1)S(1)} %collective-permute-done.from_left) | copy-start | bytes 196612
  16.8 0.6 %copy-start.1 = (bf16[16,16,128]{2,1,0:T(8,128)(2,1)}, bf16[16,16,128]{2,1,0:T(8,128)(2,1)S(1)}, u32[]{:S(2)}) copy-start(bf16[16,16,128]{2,1,0:T(8,128)(2,1)S(1)} %collective-permute-done.1.from_right) | copy-start | bytes 196612

commit v3 on v2

--- a/solution.py
+++ b/solution.py
@@ -31,6 +31,7 @@
 EDGE = 112
 INFLOW = 116
 SLOTS = 117
+GROUP = 16
 
 F32 = jnp.float32
 BF16 = jnp.bfloat16
@@ -240,8 +241,8 @@
 
 
 def halo_kernel(
-    ends, from_left, from_right, sums, inflow, solid, weights, swap, rows,
-    pay, edge, near, far, turned, back, held,
+    from_left, from_right, ends, sums, inflow, solid, weights, swap, rows,
+    pay, edge, rates, near, far, turned, back, held,
 ):
     first = lax.axis_index("space") * COLS
     last = COLS * 16 - 1
@@ -278,7 +279,9 @@
             inside = jnp.where(solid[1 - r, column] == 1, bounced, near[(1 - r) * 2 + side])
             below, above = (outside, inside) if r == 0 else (inside, outside)
             value = h - rate * h + advection(None, rows, h, left, right, below, above)
-            edge[4 + i] = jnp.where(solid[r, column] == 0, value, 0.0)
+            fluid = solid[r, column] == 0
+            edge[4 + i] = jnp.where(fluid, value, 0.0)
+            rates[i] = jnp.broadcast_to(jnp.where(fluid, rate, 0.0), (MODES, 128))
 
             inner = first if side == 0 else first + COLS - 1
             inside_band = (beyond >= 0) & (beyond <= last)
@@ -298,10 +301,19 @@
     for i in range(4):
         cell = (i // 2) * COLS + (0 if i % 2 == 0 else COLS - 1)
         later += jnp.where(place == cell, added[i * MODES : (i + 1) * MODES], 0.0)
-    out = (sums[0], later, fold(folded, 4))
+    row = lax.broadcasted_iota(jnp.int32, (64, 128), 0)
+    lane = lanes((64, 128))
+    chosen = ((lane % 32) // 4 == row % 8) & (lane % 4 == row // MODES)
+    parts = jnp.where(chosen, folded[:64], 0.0)
+    halves = []
+    for half in (0, 8):
+        total = sum(parts[i * MODES + half : i * MODES + half + 8] for i in range(4))
+        halves.append(jnp.sum(total, 0, keepdims=True))
+    ends_sums = jnp.concatenate(halves + [jnp.zeros((6, 128), F32)], 0)
     for d in range(16):
-        for i in range(3):
-            pay[d, :, 128 * i : 128 * (i + 1)] = out[i]
+        pay[d, :16, :] = sums[0]
+        pay[d, 16:32, :] = later
+        pay[d, 32:40, :] = ends_sums
 
 
 def exact_nt(value, table):
@@ -351,7 +363,7 @@
 
 
 def collide_kernel(
-    gathered, basis, projection, base_far, edge_far, cells_far, from_left, from_right, inflow,
+    gathered, basis, projection, base_far, edge_far, cells_far, rates, inflow,
     relax, flags, solid, swap_far, rows,
     out, slots, held, par, sums1, equil, wide, base, edge, cells, swap, arrived,
 ):
@@ -366,11 +378,19 @@
     first = lax.axis_index("space") * COLS
     mode = lax.axis_index("mode") * MODES
     mine = projection[pl.ds(pl.multiple_of(mode, MODES), MODES), :]
-    turned = gathered[...].T
-    node = exact_nt(turned[:128], basis[...])
-    halo_node = exact_nt(turned[256:384], basis[...])
+    now = gathered[:, :16, :].reshape(K, 128).T
+    later = gathered[:, 16:32, :].reshape(K, 128).T
+    spread = jnp.broadcast_to(gathered[:, 32:34, :].reshape(32, 1, 128), (32, 8, 128)).reshape(K, 128)
+    of_mode = lax.broadcasted_iota(jnp.int32, (K, 128), 0) % 8
+    spread = jnp.where((lanes((K, 128)) % 32) // 4 == of_mode, spread, 0.0).T
+    node = exact_nt(now, basis[...])
+    halo_node = exact_nt(spread, basis[...])
     set_parameters(par, 0, [node[32 * i : 32 * i + 32] for i in range(4)])
-    set_parameters(par, 32, [halo_node[32 * i : 32 * i + 8] for i in range(4)])
+    halo_sums = []
+    for i in range(4):
+        eight = sum(halo_node[32 * i + 8 * j : 32 * i + 8 * j + 8] for j in range(4))
+        halo_sums.append(eight + jnp.concatenate([eight[4:], eight[:4]], 0))
+    set_parameters(par, 32, halo_sums)
     slots[INFLOW] = inflow[...].astype(F32)
 
     odd = (2 * lax.broadcasted_iota(jnp.int32, (VX, K), 0) - (VX - 1)).astype(F32)
@@ -383,11 +403,11 @@
             jnp.sum(value * tri, 0, keepdims=True),
         )
 
-    def first_stage(c, carry):
+    def first_cell(c, slot):
         for r in range(ROWS):
             cell = r * COLS + c
             along_x, along_y = factors(par, cell)
-            coll = project(along_x, along_y, equil.at[r], mine)
+            coll = project(along_x, along_y, equil.at[slot + r], mine)
             fluid = solid[r, first + c] == 0
             rate = jnp.where(fluid, relax[r, c], 0.0)
             end = jnp.where(c == 0, r * 2, jnp.where(c == COLS - 1, r * 2 + 1, 8))
@@ -401,33 +421,34 @@
             sums1[pl.ds(32 + cell, 1), :] = x1 * y0
             sums1[pl.ds(64 + cell, 1), :] = x0 * y1
             sums1[pl.ds(96 + cell, 1), :] = x2 * y0 + x0 * y2
+
+    def first_stage(i, carry):
+        for u in range(GROUP):
+            first_cell(i * GROUP + u, u * ROWS)
         return carry
 
     for copy in copies:
         copy.wait()
-    lax.fori_loop(0, COLS, first_stage, 0, unroll=4)
-    for side, ref in ((0, from_left), (1, from_right)):
+    lax.fori_loop(0, COLS // GROUP, first_stage, 0)
+    for side in range(2):
         for r in range(ROWS):
             cell = HALO + r * 2 + side
-            column = jnp.clip(first - 1 if side == 0 else first + COLS, 0, COLS * 16 - 1)
-            extra = ref[r * 8 + 4].astype(F32)
-            rate = extra[:, 64:65] + extra[:, 65:66] + extra[:, 66:67]
-            rate = jnp.where(solid[r, column] == 0, rate, 0.0)
+            rate = rates[r * 2 + side][:, :1]
             along_x, along_y = factors(par, cell)
-            coll = project(along_x, along_y, equil.at[r], mine)
+            coll = project(along_x, along_y, equil.at[r * 2 + side], mine)
             slots[cell] = (edge[4 + r * 2 + side] + rate * coll).astype(BF16).astype(F32)
 
     mirrored(slots, held, OWN, swap)
-    mixed = turned[128:256] + exact_nt(sums1[...], projection[...])
+    mixed = later + exact_nt(sums1[...], projection[...])
     node = exact_nt(mixed, basis[...])
     set_parameters(par, 0, [node[32 * i : 32 * i + 32] for i in range(4)])
 
-    def second_stage(c, carry):
+    def second_cell(c, slot):
         for r in range(ROWS):
             cell = r * COLS + c
             column = first + c
             along_x, along_y = factors(par, cell)
-            coll = project(along_x, along_y, equil.at[r], mine)
+            coll = project(along_x, along_y, equil.at[slot + r], mine)
             left, right, below, above = sources(r, c, column, flags, solid)
             h = slots[cell]
             moved = advection(
@@ -438,9 +459,13 @@
             value = jnp.where(solid[r, column] == 0, value, 0.0)
             for j, (at, n) in enumerate(CHUNKS):
                 wide[j, pl.ds(cell, MODES, stride=OWN), :n] = value[:, at : at + n]
+
+    def second_stage(i, carry):
+        for u in range(GROUP):
+            second_cell(i * GROUP + u, u * ROWS)
         return carry
 
-    lax.fori_loop(0, COLS, second_stage, 0, unroll=4)
+    lax.fori_loop(0, COLS // GROUP, second_stage, 0)
     for j, (at, n) in enumerate(CHUNKS):
         out[:, :, :, at : at + n] = (
             wide[j, :, :n].astype(BF16).reshape(MODES, ROWS, COLS, n)
@@ -492,31 +517,34 @@
         ),
     )(dist, inflow, relax, flags, solid, weights, swap, rows)
 
-    pay, edge = pl.pallas_call(
+    pay, edge, rates = pl.pallas_call(
         halo_kernel,
         out_shape=(
-            jax.ShapeDtypeStruct((16, MODES, 384), F32),
+            jax.ShapeDtypeStruct((16, 40, 128), F32),
             jax.ShapeDtypeStruct((9, MODES, V), F32),
+            jax.ShapeDtypeStruct((4, MODES, 128), F32),
         ),
         in_specs=[vmem] * 5 + [smem] + [vmem] * 3,
-        out_specs=(vmem, vmem),
-        scratch_shapes=[pltpu.VMEM((4, MODES, V), F32)] * 4 + [pltpu.VMEM((192, V), BF16)],
-        compiler_params=params,
-    )(ends, from_left, from_right, sums, inflow, solid, weights, swap, rows)
+        out_specs=(vmem, vmem, vmem),
+        scratch_shapes=[pltpu.VMEM((4, MODES, V), F32)] * 4
+        + [
+            pltpu.VMEM((192, V), BF16),
+        ],
+        compiler_params=pltpu.CompilerParams(vmem_limit_bytes=63 * 1024 * 1024 + 900 * 1024),
+    )(from_left, from_right, ends, sums, inflow, solid, weights, swap, rows)
     gathered = lax.all_to_all(pay, "mode", split_axis=0, concat_axis=0, tiled=True)
-    gathered = gathered.reshape(K, 384)
 
     return pl.pallas_call(
         collide_kernel,
         out_shape=jax.ShapeDtypeStruct((MODES, ROWS, COLS, V), BF16),
-        in_specs=[vmem] * 3 + [far] * 3 + [vmem] * 3 + [smem] * 3 + [far, vmem],
+        in_specs=[vmem] * 3 + [far] * 3 + [vmem] * 2 + [smem] * 3 + [far, vmem],
         out_specs=vmem,
         scratch_shapes=[
             pltpu.VMEM((SLOTS, MODES, V), F32),
             pltpu.VMEM((576, V), BF16),
             pltpu.VMEM((4, 40, K), F32),
             pltpu.VMEM((128, K), F32),
-            pltpu.VMEM((2, V, K), BF16),
+            pltpu.VMEM((2 * GROUP, V, K), BF16),
             pltpu.VMEM((5, OWN * MODES, 128), F32),
             pltpu.VMEM((OWN, MODES, V), F32),
             pltpu.VMEM((9, MODES, V), F32),
@@ -526,7 +554,7 @@
         ],
         compiler_params=params,
     )(
-        gathered, basis, projection, base, edge, cells, from_left, from_right, inflow,
+        gathered, basis, projection, base, edge, cells, rates, inflow,
         relax, flags, solid, swap, rows,
     )
 

time: 47.4 us -> 45.3 us (0.956)
  Pallas kernels: 23 us -> 22.1 us
  blocking collectives: 14.4 us -> 13.7 us
  local copies, waits for them, and re-layouts: 0.62 us -> 0 us
    pallas_call x1, Pallas kernels: 12.8 us -> 11.9 us  [on_device(): pl.pallas_call(collide_kernel, out_shape=jax.ShapeDtypeStruct((MODES, ROW...]
    all_to_all x1, blocking collectives: 14.4 us -> 13.7 us  [on_device(): lax.all_to_all(pay, 'mode', split_axis=0, concat_axis=0, tiled=True)]
    unnamed x4 -> x0, local copies, waits for them, and re-layouts: 0.62 us -> none
  transfers between devices with their start and end apart: 2 -> 2, of which waited for: 0 -> 0; matrix products, arithmetic and copies ran while one was open for 0% -> 0% of each run, Pallas kernels for 12% -> 13%
where the time goes in v3:
time: 45.3 us; the launch traced here: 45 us
  Pallas kernels  22.1 us (49%)
  blocking collectives  13.7 us (30%)
  starting transfers between devices  9.05 us (20%)
    all_to_all x1, blocking collectives, on_device(): lax.all_to_all(pay, 'mode', split_axis=0, concat_axis=0, tiled=True)  13.7 us
    pallas_call x1, Pallas kernels, on_device(): pl.pallas_call(collide_kernel, out_shape=jax.ShapeDtypeStruct((MODES, ROW...  11.9 us
    pallas_call x1, Pallas kernels, on_device(): pl.pallas_call(explicit_kernel, out_shape=(jax.ShapeDtypeStruct((OWN, MOD...  5.8 us
    ppermute x1, starting transfers between devices, on_device(): lax.ppermute(to_left, 'space', [((i + 1) % count, i) for i in range(count)])  5.23 us
    ppermute x1, starting transfers between devices, on_device(): lax.ppermute(to_right, 'space', [(i, (i + 1) % count) for i in range(coun...  3.82 us
    pallas_call x1, Pallas kernels, on_device(): pl.pallas_call(halo_kernel, out_shape=(jax.ShapeDtypeStruct((16, 40, 128)...  2.42 us
    pallas_call x1, Pallas kernels, on_device(): pl.pallas_call(edges_kernel, out_shape=(jax.ShapeDtypeStruct((16, MODES,...  1.98 us
  transfers between devices with their start and end apart: 2, of which 0 were waited for; matrix products, arithmetic and copies ran while one was open for 0% of the time, Pallas kernels for 13%

profile of v3, /device:TPU:1, one launch (start us, length us, event | category | flops | bytes accessed | tf_op | source)
XLA Modules:
  0.0 45.0 jit_solution(12428041828510477374)
XLA Ops:
  0.0 2.0 %shard_map.100 = (bf16[16,16,128]{2,1,0:T(8,128)(2,1)}, bf16[16,16,128]{2,1,0:T(8,128)(2,1)}) custom-call(bf16[16,2,16,576]{3,2,1,0:T(8,128)(2,1)} %dist.3, f32[2,16]{1,0:T(2,128)} %relax.5, s32[2,16]{1,0:T(2,128)} %flags.5), custom_call_target="tpu_custom_call" | custom-call | tf_op jit(solution)/shard_map/pallas_call | solution.py:482
  2.0 3.8 %collective-permute-start = (bf16[16,16,128]{2,1,0:T(8,128)(2,1)}, bf16[16,16,128]{2,1,0:T(8,128)(2,1)}, u32[]{:S(2)}, u32[]{:S(2)}) collective-permute-start(bf16[16,16,128]{2,1,0:T(8,128)(2,1)} %get-tuple-element.14), channel_id=1, source_target_pairs={{0,16},{16,32},{32,48},{48,64},{64,80},{80,96},{96,112},{112,128},... | collective-permute-start | bytes 196616 | tf_op jit(solution)/shard_map/ppermute | solution.py:494
  5.8 5.2 %collective-permute-start.1 = (bf16[16,16,128]{2,1,0:T(8,128)(2,1)}, bf16[16,16,128]{2,1,0:T(8,128)(2,1)}, u32[]{:S(2)}, u32[]{:S(2)}) collective-permute-start(bf16[16,16,128]{2,1,0:T(8,128)(2,1)} %get-tuple-element.15), channel_id=1, source_target_pairs={{16,0},{32,16},{48,32},{64,48},{80,64},{96,80},{112,96},{128,112},... | collective-permute-start | bytes 196616 | tf_op jit(solution)/shard_map/ppermute | solution.py:495
  11.0 5.8 %shard_map.101 = (bf16[32,16,576]{2,1,0:T(8,128)(2,1)}, bf16[4,16,576]{2,1,0:T(8,128)(2,1)}, f32[32,16,576]{2,1,0:T(8,128)}, f32[2,16,128]{2,1,0:T(8,128)}) custom-call(bf16[16,2,16,576]{3,2,1,0:T(8,128)(2,1)} %dist.3, bf16[16,576]{1,0:T(8,128)(2,1)} %inflow.5, f32[2,16]{1,0:T(2,128)} %relax.5, s32[2,16]{1,0:T(2,128)} %flags.5, s32[2,256]{1,0:T(2,128)} %solid.5, ...), custom_call_target="tpu_custom_call" | custom-call | flops 20000000000 | bytes 4000000 | tf_op jit(solution)/shard_map/pallas_call | solution.py:497
  16.8 0.0 collective-permute-done.from_left
  16.8 0.0 collective-permute-done.1.from_right
  16.8 2.4 %shard_map.102 = (f32[16,40,128]{2,1,0:T(8,128)}, f32[9,16,576]{2,1,0:T(8,128)}, f32[4,16,128]{2,1,0:T(8,128)}) custom-call(bf16[16,16,128]{2,1,0:T(8,128)(2,1)} %collective-permute-done.from_left, bf16[16,16,128]{2,1,0:T(8,128)(2,1)} %collective-permute-done.1.from_right, bf16[4,16,576]{2,1,0:T(8,128)(2,1)} %get-tuple-element.16.ends, ...), custom_call_target="tpu_custom_call" | custom-call | tf_op jit(solution)/shard_map/pallas_call | solution.py:520
  19.3 13.7 %all_to_all.5.gathered = f32[16,40,128]{2,1,0:T(8,128)} all-to-all(f32[16,40,128]{2,1,0:T(8,128)} %get-tuple-element.18), channel_id=1, replica_groups=mesh['space'=16,'mode'=16] {'mode'}, dimensions={0} | all-to-all | bytes 655360 | tf_op jit(solution)/shard_map/all_to_all | solution.py:535
  32.9 11.9 %shard_map.103 = bf16[16,2,16,576]{3,2,1,0:T(8,128)(2,1)} custom-call(f32[16,40,128]{2,1,0:T(8,128)} %all_to_all.5.gathered, bf16[256,256]{1,0:T(8,128)(2,1)} %basis.1, bf16[256,256]{1,0:T(8,128)(2,1)} %projection.1, f32[32,16,576]{2,1,0:T(8,128)} %get-tuple-element.19.base_far, f32[9,16,576]{2,1,0:T(8,128)} %get-tuple-element.20.edge_far, ...), custom_call_target="tpu_custom_call" | custom-call | tf_op jit(solution)/shard_map/pallas_call | solution.py:537
Async XLA Ops:
  2.0 14.9 %collective-permute-start = (bf16[16,16,128]{2,1,0:T(8,128)(2,1)}, bf16[16,16,128]{2,1,0:T(8,128)(2,1)}, u32[]{:S(2)}, u32[]{:S(2)}) collective-permute-start(bf16[16,16,128]{2,1,0:T(8,128)(2,1)} %get-tuple-element.14), channel_id=1, source_target_pairs={{0,16},{16,32},{32,48},{48,64},{64,80},{80,96},{96,112},{112,128},... | collective-permute-start | bytes 196616 | tf_op jit(solution)/shard_map/ppermute | solution.py:494
  5.8 11.0 %collective-permute-start.1 = (bf16[16,16,128]{2,1,0:T(8,128)(2,1)}, bf16[16,16,128]{2,1,0:T(8,128)(2,1)}, u32[]{:S(2)}, u32[]{:S(2)}) collective-permute-start(bf16[16,16,128]{2,1,0:T(8,128)(2,1)} %get-tuple-element.15), channel_id=1, source_target_pairs={{16,0},{32,16},{48,32},{64,48},{80,64},{96,80},{112,96},{128,112},... | collective-permute-start | bytes 196616 | tf_op jit(solution)/shard_map/ppermute | solution.py:495

commit v4 on v3

--- a/solution.py
+++ b/solution.py
@@ -53,6 +53,9 @@
     swap[191 - lane, lane] = 1.0
     for at, left, out in ((256, 0, 0), (512, 0, 128), (896, 128, 256)):
         swap[at + turned[out + lane] - left, lane] = 1.0
+    pair = np.arange(256)
+    order = np.zeros((256, 256), np.float32)
+    order[pair, pair % 16 * 16 + pair // 16] = 1.0
     rows = np.zeros((8, V), np.float32)
     rows[0] = DT_DX * np.abs(-VMAX + STEP * a)
     rows[1] = DT_DX * np.abs(-VMAX + STEP * b)
@@ -62,6 +65,7 @@
         jnp.asarray(weights.astype(np.float32), BF16),
         jnp.asarray(swap, BF16),
         jnp.asarray(rows),
+        jnp.asarray(order, BF16),
     )
 
 
@@ -189,25 +193,21 @@
     low[pl.ds(at, MODES), :] = (value - hi.astype(F32)).astype(BF16)
 
 
+def by_other(value, order):
+    return jnp.dot(order[...], value, preferred_element_type=F32)
+
+
 def explicit_kernel(
-    dist, inflow, relax, flags, solid, weights, swap, rows,
-    cells, ends, base, sums, wide, slots, held, high, low,
+    dist, inflow, relax, flags, solid, weights, swap, rows, order,
+    cells, ends, base, sums, slots, held, high, low,
 ):
     first = lax.axis_index("space") * COLS
-    widen(dist, wide)
-
-    def gather(c, carry):
-        for r in range(ROWS):
-            cell = r * COLS + c
-            at_held = pl.multiple_of(cell * MODES, MODES)
-            for j, (at, n) in enumerate(CHUNKS):
-                value = cell_chunk(wide, cell, j)[:, :n]
-                slots[cell, :, at : at + n] = value
-                held[pl.ds(at_held, MODES), at : at + n] = value.astype(BF16)
-        return carry
-
-    lax.fori_loop(0, COLS, gather, 0, unroll=2)
-    cells[...] = held[: OWN * MODES, :].reshape(OWN, MODES, V)
+    for r in range(ROWS):
+        top = r * COLS
+        value = by_other(dist[:, r, :, :].reshape(COLS * MODES, V), order)
+        slots[top : top + COLS] = value.reshape(COLS, MODES, V)
+        held[top * MODES : (top + COLS) * MODES, :] = value.astype(BF16)
+    cells[...] = held[: OWN * MODES, :]
     for e, cell in enumerate((0, COLS - 1, COLS, 2 * COLS - 1)):
         ends[e] = held[cell * MODES : (cell + 1) * MODES, :]
     slots[INFLOW] = inflow[...].astype(F32)
@@ -318,7 +318,7 @@
 
 def exact_nt(value, table):
     total = None
-    for piece in pieces(value):
+    for piece in pieces(value)[:2]:
         part = lax.dot_general(piece, table, NT, preferred_element_type=F32)
         total = part if total is None else total + part
     return total
@@ -364,8 +364,8 @@
 
 def collide_kernel(
     gathered, basis, projection, base_far, edge_far, cells_far, rates, inflow,
-    relax, flags, solid, swap_far, rows,
-    out, slots, held, par, sums1, equil, wide, base, edge, cells, swap, arrived,
+    relax, flags, solid, swap_far, rows, order,
+    out, slots, held, par, sums1, equil, base, edge, cells, swap, arrived, ready, written,
 ):
     copies = [
         pltpu.make_async_copy(source, target, arrived.at[i])
@@ -443,37 +443,35 @@
     node = exact_nt(mixed, basis[...])
     set_parameters(par, 0, [node[32 * i : 32 * i + 32] for i in range(4)])
 
-    def second_cell(c, slot):
-        for r in range(ROWS):
+    writes = []
+    for r in range(ROWS):
+        for c in range(COLS):
             cell = r * COLS + c
             column = first + c
             along_x, along_y = factors(par, cell)
-            coll = project(along_x, along_y, equil.at[slot + r], mine)
+            coll = project(along_x, along_y, equil.at[cell], mine)
             left, right, below, above = sources(r, c, column, flags, solid)
             h = slots[cell]
             moved = advection(
                 slots, rows, h, slots[left], slots[right], slots[below], slots[above]
             )
             value = h + moved + relax[r, c] * (coll - h)
-            value = 0.5 * cells[cell].astype(F32) + 0.5 * value
+            before = cells[cell * MODES : (cell + 1) * MODES, :].astype(F32)
+            value = 0.5 * before + 0.5 * value
             value = jnp.where(solid[r, column] == 0, value, 0.0)
-            for j, (at, n) in enumerate(CHUNKS):
-                wide[j, pl.ds(cell, MODES, stride=OWN), :n] = value[:, at : at + n]
-
-    def second_stage(i, carry):
-        for u in range(GROUP):
-            second_cell(i * GROUP + u, u * ROWS)
-        return carry
-
-    lax.fori_loop(0, COLS // GROUP, second_stage, 0)
-    for j, (at, n) in enumerate(CHUNKS):
-        out[:, :, :, at : at + n] = (
-            wide[j, :, :n].astype(BF16).reshape(MODES, ROWS, COLS, n)
-        )
+            held[cell * MODES : (cell + 1) * MODES, :] = value.astype(BF16)
+        top = r * COLS * MODES
+        value = by_other(held[top : top + COLS * MODES, :], order)
+        ready[:, r, :, :] = value.astype(BF16).reshape(MODES, COLS, V)
+        write = pltpu.make_async_copy(ready.at[:, r], out.at[:, r], written.at[r])
+        write.start()
+        writes.append(write)
+    for write in writes:
+        write.wait()
 
 
 def on_device(dist, relax, flags, solid, inflow, basis, projection):
-    weights, swap, rows = tables()
+    weights, swap, rows, order = tables()
     vmem = pl.BlockSpec(memory_space=pltpu.VMEM)
     smem = pl.BlockSpec(memory_space=pltpu.SMEM)
     far = pl.BlockSpec(memory_space=pl.ANY)
@@ -497,15 +495,14 @@
     cells, ends, base, sums = pl.pallas_call(
         explicit_kernel,
         out_shape=(
-            jax.ShapeDtypeStruct((OWN, MODES, V), BF16),
+            jax.ShapeDtypeStruct((OWN * MODES, V), BF16),
             jax.ShapeDtypeStruct((4, MODES, V), BF16),
             jax.ShapeDtypeStruct((OWN, MODES, V), F32),
             jax.ShapeDtypeStruct((2, MODES, 128), F32),
         ),
-        in_specs=[vmem] * 2 + [smem] * 3 + [vmem] * 3,
+        in_specs=[vmem] * 2 + [smem] * 3 + [vmem] * 4,
         out_specs=(vmem, vmem, vmem, vmem),
         scratch_shapes=[
-            pltpu.VMEM((5, OWN * MODES, 128), F32),
             pltpu.VMEM((SLOTS, MODES, V), F32),
             pltpu.VMEM((576, V), BF16),
             pltpu.VMEM((OWN * MODES, V), BF16),
@@ -515,7 +512,7 @@
         cost_estimate=pl.CostEstimate(
             flops=20_000_000_000, bytes_accessed=4_000_000, transcendentals=0
         ),
-    )(dist, inflow, relax, flags, solid, weights, swap, rows)
+    )(dist, inflow, relax, flags, solid, weights, swap, rows, order)
 
     pay, edge, rates = pl.pallas_call(
         halo_kernel,
@@ -537,25 +534,26 @@
     return pl.pallas_call(
         collide_kernel,
         out_shape=jax.ShapeDtypeStruct((MODES, ROWS, COLS, V), BF16),
-        in_specs=[vmem] * 3 + [far] * 3 + [vmem] * 2 + [smem] * 3 + [far, vmem],
-        out_specs=vmem,
+        in_specs=[vmem] * 3 + [far] * 3 + [vmem] * 2 + [smem] * 3 + [far, vmem, vmem],
+        out_specs=far,
         scratch_shapes=[
             pltpu.VMEM((SLOTS, MODES, V), F32),
             pltpu.VMEM((576, V), BF16),
             pltpu.VMEM((4, 40, K), F32),
             pltpu.VMEM((128, K), F32),
             pltpu.VMEM((2 * GROUP, V, K), BF16),
-            pltpu.VMEM((5, OWN * MODES, 128), F32),
             pltpu.VMEM((OWN, MODES, V), F32),
             pltpu.VMEM((9, MODES, V), F32),
-            pltpu.VMEM((OWN, MODES, V), BF16),
+            pltpu.VMEM((OWN * MODES, V), BF16),
             pltpu.VMEM((1152, 128), BF16),
             pltpu.SemaphoreType.DMA((4,)),
+            pltpu.VMEM((MODES, ROWS, COLS, V), BF16),
+            pltpu.SemaphoreType.DMA((ROWS,)),
         ],
         compiler_params=params,
     )(
         gathered, basis, projection, base, edge, cells, rates, inflow,
-        relax, flags, solid, swap, rows,
+        relax, flags, solid, swap, rows, order,
     )
 
 

time: 45.3 us -> 43.5 us (0.960)
  Pallas kernels: 22.1 us -> 20.4 us
    pallas_call x1, Pallas kernels: 5.8 us -> 4.86 us  [on_device(): pl.pallas_call(explicit_kernel, out_shape=(jax.ShapeDtypeStruct((OWN * MO...]
    pallas_call x1, Pallas kernels: 11.9 us -> 11.2 us  [on_device(): pl.pallas_call(collide_kernel, out_shape=jax.ShapeDtypeStruct((MODES, ROW...]
  transfers between devices with their start and end apart: 2 -> 2, of which waited for: 0 -> 0; matrix products, arithmetic and copies ran while one was open for 0% -> 0% of each run, Pallas kernels for 13% -> 11%
where the time goes in v4:
time: 43.5 us; the launch traced here: 43.2 us
  Pallas kernels  20.4 us (47%)
  blocking collectives  13.7 us (31%)
  starting transfers between devices  9.05 us (21%)
    all_to_all x1, blocking collectives, on_device(): lax.all_to_all(pay, 'mode', split_axis=0, concat_axis=0, tiled=True)  13.7 us
    pallas_call x1, Pallas kernels, on_device(): pl.pallas_call(collide_kernel, out_shape=jax.ShapeDtypeStruct((MODES, ROW...  11.2 us
    ppermute x1, starting transfers between devices, on_device(): lax.ppermute(to_left, 'space', [((i + 1) % count, i) for i in range(count)])  5.23 us
    pallas_call x1, Pallas kernels, on_device(): pl.pallas_call(explicit_kernel, out_shape=(jax.ShapeDtypeStruct((OWN * MO...  4.86 us
    ppermute x1, starting transfers between devices, on_device(): lax.ppermute(to_right, 'space', [(i, (i + 1) % count) for i in range(coun...  3.82 us
    pallas_call x1, Pallas kernels, on_device(): pl.pallas_call(halo_kernel, out_shape=(jax.ShapeDtypeStruct((16, 40, 128)...  2.42 us
    pallas_call x1, Pallas kernels, on_device(): pl.pallas_call(edges_kernel, out_shape=(jax.ShapeDtypeStruct((16, MODES,...  1.98 us
  transfers between devices with their start and end apart: 2, of which 0 were waited for; matrix products, arithmetic and copies ran while one was open for 0% of the time, Pallas kernels for 11%

profile of v4, /device:TPU:1, one launch (start us, length us, event | category | flops | bytes accessed | tf_op | source)
XLA Modules:
  0.0 43.2 jit_solution(16180134122790039852)
XLA Ops:
  0.0 2.0 %shard_map.109 = (bf16[16,16,128]{2,1,0:T(8,128)(2,1)}, bf16[16,16,128]{2,1,0:T(8,128)(2,1)}) custom-call(bf16[16,2,16,576]{3,2,1,0:T(8,128)(2,1)} %dist.3, f32[2,16]{1,0:T(2,128)} %relax.5, s32[2,16]{1,0:T(2,128)} %flags.5), custom_call_target="tpu_custom_call" | custom-call | tf_op jit(solution)/shard_map/pallas_call | solution.py:480
  2.0 3.8 %collective-permute-start = (bf16[16,16,128]{2,1,0:T(8,128)(2,1)}, bf16[16,16,128]{2,1,0:T(8,128)(2,1)}, u32[]{:S(2)}, u32[]{:S(2)}) collective-permute-start(bf16[16,16,128]{2,1,0:T(8,128)(2,1)} %get-tuple-element.14), channel_id=1, source_target_pairs={{0,16},{16,32},{32,48},{48,64},{64,80},{80,96},{96,112},{112,128},... | collective-permute-start | bytes 196616 | tf_op jit(solution)/shard_map/ppermute | solution.py:492
  5.8 5.2 %collective-permute-start.1 = (bf16[16,16,128]{2,1,0:T(8,128)(2,1)}, bf16[16,16,128]{2,1,0:T(8,128)(2,1)}, u32[]{:S(2)}, u32[]{:S(2)}) collective-permute-start(bf16[16,16,128]{2,1,0:T(8,128)(2,1)} %get-tuple-element.15), channel_id=1, source_target_pairs={{16,0},{32,16},{48,32},{64,48},{80,64},{96,80},{112,96},{128,112},... | collective-permute-start | bytes 196616 | tf_op jit(solution)/shard_map/ppermute | solution.py:493
  11.0 4.9 %shard_map.110 = (bf16[512,576]{1,0:T(8,128)(2,1)}, bf16[4,16,576]{2,1,0:T(8,128)(2,1)}, f32[32,16,576]{2,1,0:T(8,128)}, f32[2,16,128]{2,1,0:T(8,128)}) custom-call(bf16[16,2,16,576]{3,2,1,0:T(8,128)(2,1)} %dist.3, bf16[16,576]{1,0:T(8,128)(2,1)} %inflow.5, f32[2,16]{1,0:T(2,128)} %relax.5, s32[2,16]{1,0:T(2,128)} %flags.5, s32[2,256]{1,0:T(2,128)} %solid.5, ...), custom_call_target="tpu_custom_call" | custom-call | flops 20000000000 | bytes 4000000 | tf_op jit(solution)/shard_map/pallas_call | solution.py:495
  15.9 0.0 collective-permute-done.from_left
  15.9 0.0 collective-permute-done.1.from_right
  15.9 2.4 %shard_map.111 = (f32[16,40,128]{2,1,0:T(8,128)}, f32[9,16,576]{2,1,0:T(8,128)}, f32[4,16,128]{2,1,0:T(8,128)}) custom-call(bf16[16,16,128]{2,1,0:T(8,128)(2,1)} %collective-permute-done.from_left, bf16[16,16,128]{2,1,0:T(8,128)(2,1)} %collective-permute-done.1.from_right, bf16[4,16,576]{2,1,0:T(8,128)(2,1)} %get-tuple-element.16.ends, ...), custom_call_target="tpu_custom_call" | custom-call | tf_op jit(solution)/shard_map/pallas_call | solution.py:517
  18.3 13.7 %all_to_all.5.gathered = f32[16,40,128]{2,1,0:T(8,128)} all-to-all(f32[16,40,128]{2,1,0:T(8,128)} %get-tuple-element.18), channel_id=1, replica_groups=mesh['space'=16,'mode'=16] {'mode'}, dimensions={0} | all-to-all | bytes 655360 | tf_op jit(solution)/shard_map/all_to_all | solution.py:532
  32.0 11.2 %shard_map.112 = bf16[16,2,16,576]{3,2,1,0:T(8,128)(2,1)} custom-call(f32[16,40,128]{2,1,0:T(8,128)} %all_to_all.5.gathered, bf16[256,256]{1,0:T(8,128)(2,1)} %basis.1, bf16[256,256]{1,0:T(8,128)(2,1)} %projection.1, f32[32,16,576]{2,1,0:T(8,128)} %get-tuple-element.19.base_far, f32[9,16,576]{2,1,0:T(8,128)} %get-tuple-element.20.edge_far, ...), custom_call_target="tpu_custom_call" | custom-call | tf_op jit(solution)/shard_map/pallas_call | solution.py:534
Async XLA Ops:
  2.0 13.9 %collective-permute-start = (bf16[16,16,128]{2,1,0:T(8,128)(2,1)}, bf16[16,16,128]{2,1,0:T(8,128)(2,1)}, u32[]{:S(2)}, u32[]{:S(2)}) collective-permute-start(bf16[16,16,128]{2,1,0:T(8,128)(2,1)} %get-tuple-element.14), channel_id=1, source_target_pairs={{0,16},{16,32},{32,48},{48,64},{64,80},{80,96},{96,112},{112,128},... | collective-permute-start | bytes 196616 | tf_op jit(solution)/shard_map/ppermute | solution.py:492
  5.8 10.1 %collective-permute-start.1 = (bf16[16,16,128]{2,1,0:T(8,128)(2,1)}, bf16[16,16,128]{2,1,0:T(8,128)(2,1)}, u32[]{:S(2)}, u32[]{:S(2)}) collective-permute-start(bf16[16,16,128]{2,1,0:T(8,128)(2,1)} %get-tuple-element.15), channel_id=1, source_target_pairs={{16,0},{32,16},{48,32},{64,48},{80,64},{96,80},{112,96},{128,112},... | collective-permute-start | bytes 196616 | tf_op jit(solution)/shard_map/ppermute | solution.py:493

commit v5 on v4

--- a/solution.py
+++ b/solution.py
@@ -66,6 +66,7 @@
         jnp.asarray(swap, BF16),
         jnp.asarray(rows),
         jnp.asarray(order, BF16),
+        jnp.asarray(np.concatenate([order[:32], order[224:]]), BF16),
     )
 
 
@@ -81,20 +82,14 @@
     return hi, mid, low
 
 
-def cell_chunk(wide, cell, j):
-    return wide[j, pl.ds(cell, MODES, stride=OWN), :]
-
-
-def widen(dist, wide):
-    for j, (at, n) in enumerate(CHUNKS):
-        wide[j, :, :n] = dist[:, :, :, at : at + n].reshape(ROWS * COLS * MODES, n).astype(F32)
-
-
-def edges_kernel(dist, relax, flags, to_left, to_right, wide):
-    widen(dist, wide)
+def edges_kernel(dist, relax, flags, pick, to_left, to_right):
     lane = lanes((MODES, 128))
-    for out, near, far, first in ((to_left, 0, 1, 0), (to_right, COLS - 1, COLS - 2, 2)):
-        for r in range(ROWS):
+    for r in range(ROWS):
+        taken = by_other(dist[:, r, :, :].reshape(COLS * MODES, V), pick)
+        for out, near, at_near, at_far, first in (
+            (to_left, 0, 0, 1, 0),
+            (to_right, COLS - 1, 3, 2, 2),
+        ):
             hi, mid, low = pieces(jnp.full((MODES, 128), relax[r, near], F32))
             flag = jnp.full((MODES, 128), flags[r, near], jnp.int32).astype(F32)
             extra = jnp.where(
@@ -106,15 +101,16 @@
                     jnp.where(lane == 66, low.astype(F32), jnp.where(lane == 67, flag, 0.0)),
                 ),
             )
-            for j in range(5):
-                value = cell_chunk(wide, r * COLS + near, j)
+            for j, (at, n) in enumerate(CHUNKS):
+                value = taken[at_near * MODES : (at_near + 1) * MODES, at : at + n]
                 if j == 4:
-                    value = jnp.where(lane < 64, value, extra)
+                    value = jnp.concatenate([value, extra[:, n:]], 1)
                 out[r * 8 + j] = value.astype(BF16)
             for j in range(3):
-                value = cell_chunk(wide, r * COLS + far, first + j)
-                if first + j == 4:
-                    value = jnp.where(lane < 64, value, 0.0)
+                at, n = CHUNKS[first + j]
+                value = taken[at_far * MODES : (at_far + 1) * MODES, at : at + n]
+                if n < 128:
+                    value = jnp.concatenate([value, jnp.zeros((MODES, 128 - n), F32)], 1)
                 out[r * 8 + 5 + j] = value.astype(BF16)
 
 
@@ -352,13 +348,11 @@
     return scale * jnp.exp2(dx * dx * rate), jnp.exp2(dy * dy * rate)
 
 
-def project(along_x, along_y, equil, projection):
-    for i in range(VX // 2):
-        pair = jnp.concatenate(
-            [along_x[2 * i : 2 * i + 1] * along_y, along_x[2 * i + 1 : 2 * i + 2] * along_y], 0
-        )
-        equil[48 * i : 48 * (i + 1), :] = pair.astype(BF16)
-    out = lax.dot_general(projection, equil[...], NT, preferred_element_type=F32)
+def project(along_x, along_y, scaled, projection):
+    for i in range(VX):
+        scaled[MODES * i : MODES * (i + 1), :] = (projection * along_x[i : i + 1]).astype(BF16)
+    out = lax.dot_general(scaled[...], along_y.astype(BF16), NT, preferred_element_type=F32)
+    out = jnp.concatenate([out[MODES * i : MODES * (i + 1)] for i in range(VX)], 1)
     return out.astype(BF16).astype(F32)
 
 
@@ -377,7 +371,7 @@
         copy.start()
     first = lax.axis_index("space") * COLS
     mode = lax.axis_index("mode") * MODES
-    mine = projection[pl.ds(pl.multiple_of(mode, MODES), MODES), :]
+    mine = projection[pl.ds(pl.multiple_of(mode, MODES), MODES), :].astype(F32)
     now = gathered[:, :16, :].reshape(K, 128).T
     later = gathered[:, 16:32, :].reshape(K, 128).T
     spread = jnp.broadcast_to(gathered[:, 32:34, :].reshape(32, 1, 128), (32, 8, 128)).reshape(K, 128)
@@ -471,7 +465,7 @@
 
 
 def on_device(dist, relax, flags, solid, inflow, basis, projection):
-    weights, swap, rows, order = tables()
+    weights, swap, rows, order, pick = tables()
     vmem = pl.BlockSpec(memory_space=pltpu.VMEM)
     smem = pl.BlockSpec(memory_space=pltpu.SMEM)
     far = pl.BlockSpec(memory_space=pl.ANY)
@@ -483,11 +477,10 @@
             jax.ShapeDtypeStruct((16, MODES, 128), BF16),
             jax.ShapeDtypeStruct((16, MODES, 128), BF16),
         ),
-        in_specs=[vmem, smem, smem],
+        in_specs=[vmem, smem, smem, vmem],
         out_specs=(vmem, vmem),
-        scratch_shapes=[pltpu.VMEM((5, OWN * MODES, 128), F32)],
         compiler_params=params,
-    )(dist, relax, flags)
+    )(dist, relax, flags, pick)
     count = lax.axis_size("space")
     from_left = lax.ppermute(to_right, "space", [(i, (i + 1) % count) for i in range(count)])
     from_right = lax.ppermute(to_left, "space", [((i + 1) % count, i) for i in range(count)])
@@ -541,7 +534,7 @@
             pltpu.VMEM((576, V), BF16),
             pltpu.VMEM((4, 40, K), F32),
             pltpu.VMEM((128, K), F32),
-            pltpu.VMEM((2 * GROUP, V, K), BF16),
+            pltpu.VMEM((2 * GROUP, VX * MODES, K), BF16),
             pltpu.VMEM((OWN, MODES, V), F32),
             pltpu.VMEM((9, MODES, V), F32),
             pltpu.VMEM((OWN * MODES, V), BF16),

time: 43.5 us -> 42.7 us (0.982)
  Pallas kernels: 20.4 us -> 19.7 us
    pallas_call x1, Pallas kernels: 11.2 us -> 10.4 us  [on_device(): pl.pallas_call(collide_kernel, out_shape=jax.ShapeDtypeStruct((MODES, ROW...]
where the time goes in v5:
time: 42.7 us; the launch traced here: 42.4 us
  Pallas kernels  19.7 us (46%)
  blocking collectives  13.7 us (32%)
  starting transfers between devices  9.05 us (21%)
    all_to_all x1, blocking collectives, on_device(): lax.all_to_all(pay, 'mode', split_axis=0, concat_axis=0, tiled=True)  13.7 us
    pallas_call x1, Pallas kernels, on_device(): pl.pallas_call(collide_kernel, out_shape=jax.ShapeDtypeStruct((MODES, ROW...  10.4 us
    ppermute x1, starting transfers between devices, on_device(): lax.ppermute(to_left, 'space', [((i + 1) % count, i) for i in range(count)])  5.23 us
    pallas_call x1, Pallas kernels, on_device(): pl.pallas_call(explicit_kernel, out_shape=(jax.ShapeDtypeStruct((OWN * MO...  4.87 us
    ppermute x1, starting transfers between devices, on_device(): lax.ppermute(to_right, 'space', [(i, (i + 1) % count) for i in range(coun...  3.82 us
    pallas_call x1, Pallas kernels, on_device(): pl.pallas_call(halo_kernel, out_shape=(jax.ShapeDtypeStruct((16, 40, 128)...  2.42 us
    pallas_call x1, Pallas kernels, on_device(): pl.pallas_call(edges_kernel, out_shape=(jax.ShapeDtypeStruct((16, MODES,...  1.96 us
  transfers between devices with their start and end apart: 2, of which 0 were waited for; matrix products, arithmetic and copies ran while one was open for 0% of the time, Pallas kernels for 11%

profile of v5, /device:TPU:1, one launch (start us, length us, event | category | flops | bytes accessed | tf_op | source)
XLA Modules:
  0.0 42.4 jit_solution(13039577043676101783)
XLA Ops:
  0.0 2.0 %shard_map.118 = (bf16[16,16,128]{2,1,0:T(8,128)(2,1)}, bf16[16,16,128]{2,1,0:T(8,128)(2,1)}) custom-call(bf16[16,2,16,576]{3,2,1,0:T(8,128)(2,1)} %dist.3, f32[2,16]{1,0:T(2,128)} %relax.5, s32[2,16]{1,0:T(2,128)} %flags.5, bf16[64,256]{1,0:T(8,128)(2,1)} %constant.14.clone.pick), custom_call_target="tpu_custom_call" | custom-call | tf_op jit(solution)/shard_map/pallas_call | solution.py:474
  2.0 3.8 %collective-permute-start = (bf16[16,16,128]{2,1,0:T(8,128)(2,1)}, bf16[16,16,128]{2,1,0:T(8,128)(2,1)}, u32[]{:S(2)}, u32[]{:S(2)}) collective-permute-start(bf16[16,16,128]{2,1,0:T(8,128)(2,1)} %get-tuple-element.14), channel_id=1, source_target_pairs={{0,16},{16,32},{32,48},{48,64},{64,80},{80,96},{96,112},{112,128},... | collective-permute-start | bytes 196616 | tf_op jit(solution)/shard_map/ppermute | solution.py:485
  5.8 5.2 %collective-permute-start.1 = (bf16[16,16,128]{2,1,0:T(8,128)(2,1)}, bf16[16,16,128]{2,1,0:T(8,128)(2,1)}, u32[]{:S(2)}, u32[]{:S(2)}) collective-permute-start(bf16[16,16,128]{2,1,0:T(8,128)(2,1)} %get-tuple-element.15), channel_id=1, source_target_pairs={{16,0},{32,16},{48,32},{64,48},{80,64},{96,80},{112,96},{128,112},... | collective-permute-start | bytes 196616 | tf_op jit(solution)/shard_map/ppermute | solution.py:486
  11.0 4.9 %shard_map.119 = (bf16[512,576]{1,0:T(8,128)(2,1)}, bf16[4,16,576]{2,1,0:T(8,128)(2,1)}, f32[32,16,576]{2,1,0:T(8,128)}, f32[2,16,128]{2,1,0:T(8,128)}) custom-call(bf16[16,2,16,576]{3,2,1,0:T(8,128)(2,1)} %dist.3, bf16[16,576]{1,0:T(8,128)(2,1)} %inflow.5, f32[2,16]{1,0:T(2,128)} %relax.5, s32[2,16]{1,0:T(2,128)} %flags.5, s32[2,256]{1,0:T(2,128)} %solid.5, ...), custom_call_target="tpu_custom_call" | custom-call | flops 20000000000 | bytes 4000000 | tf_op jit(solution)/shard_map/pallas_call | solution.py:488
  15.9 0.0 collective-permute-done.from_left
  15.9 0.0 collective-permute-done.1.from_right
  15.9 2.4 %shard_map.120 = (f32[16,40,128]{2,1,0:T(8,128)}, f32[9,16,576]{2,1,0:T(8,128)}, f32[4,16,128]{2,1,0:T(8,128)}) custom-call(bf16[16,16,128]{2,1,0:T(8,128)(2,1)} %collective-permute-done.from_left, bf16[16,16,128]{2,1,0:T(8,128)(2,1)} %collective-permute-done.1.from_right, bf16[4,16,576]{2,1,0:T(8,128)(2,1)} %get-tuple-element.16.ends, ...), custom_call_target="tpu_custom_call" | custom-call | tf_op jit(solution)/shard_map/pallas_call | solution.py:510
  18.3 13.7 %all_to_all.5.gathered = f32[16,40,128]{2,1,0:T(8,128)} all-to-all(f32[16,40,128]{2,1,0:T(8,128)} %get-tuple-element.18), channel_id=1, replica_groups=mesh['space'=16,'mode'=16] {'mode'}, dimensions={0} | all-to-all | bytes 655360 | tf_op jit(solution)/shard_map/all_to_all | solution.py:525
  32.0 10.4 %shard_map.121 = bf16[16,2,16,576]{3,2,1,0:T(8,128)(2,1)} custom-call(f32[16,40,128]{2,1,0:T(8,128)} %all_to_all.5.gathered, bf16[256,256]{1,0:T(8,128)(2,1)} %basis.1, bf16[256,256]{1,0:T(8,128)(2,1)} %projection.1, f32[32,16,576]{2,1,0:T(8,128)} %get-tuple-element.19.base_far, f32[9,16,576]{2,1,0:T(8,128)} %get-tuple-element.20.edge_far, ...), custom_call_target="tpu_custom_call" | custom-call | tf_op jit(solution)/shard_map/pallas_call | solution.py:527
Async XLA Ops:
  2.0 13.9 %collective-permute-start = (bf16[16,16,128]{2,1,0:T(8,128)(2,1)}, bf16[16,16,128]{2,1,0:T(8,128)(2,1)}, u32[]{:S(2)}, u32[]{:S(2)}) collective-permute-start(bf16[16,16,128]{2,1,0:T(8,128)(2,1)} %get-tuple-element.14), channel_id=1, source_target_pairs={{0,16},{16,32},{32,48},{48,64},{64,80},{80,96},{96,112},{112,128},... | collective-permute-start | bytes 196616 | tf_op jit(solution)/shard_map/ppermute | solution.py:485
  5.8 10.1 %collective-permute-start.1 = (bf16[16,16,128]{2,1,0:T(8,128)(2,1)}, bf16[16,16,128]{2,1,0:T(8,128)(2,1)}, u32[]{:S(2)}, u32[]{:S(2)}) collective-permute-start(bf16[16,16,128]{2,1,0:T(8,128)(2,1)} %get-tuple-element.15), channel_id=1, source_target_pairs={{16,0},{32,16},{48,32},{64,48},{80,64},{96,80},{112,96},{128,112},... | collective-permute-start | bytes 196616 | tf_op jit(solution)/shard_map/ppermute | solution.py:486
